TPU v7x, 32 devices: a whole 2x2x4 slice. The times are simulated.
32 devices in a mesh: grp: 2 (over x), ch: 16 (over z, y, core).
Axes of the slice: x: 2, y: 2, z: 4, core: 2. Of those that a mesh axis runs over, the one named last changes fastest.
Arguments:
- features: bfloat16 [2048, 2048], P('ch', 'grp'), parts along dimension 1, may hold values from -50 to 50
- dw_weight: float32 [2048, 49], P('ch'), may hold values from -0.875 to 0.875
- norm_gain: float32 [2048], replicated, may hold values from 0.25 to 1.75
- layer_scale: float32 [2048], replicated, may hold values from 0.2 to 1
- w_in: bfloat16 [8192, 2048], P('ch'), may hold values from -0.125 to 0.125
- w_out: bfloat16 [8192, 2048], P('ch'), may hold values from -0.0625 to 0.0625
- w_head: bfloat16 [2048, 150], replicated, may hold values from -3 to 3
- labels: int32 [2048], P('grp'), parts along dimension 0, may hold values from 0 to 149
Outputs:
- d_features: float32 [2048, 2048], P('ch', 'grp'), parts along dimension 1
- d_dw: float32 [2048, 98], P('ch', 'grp'), parts along dimension 1
- d_scale: float32 [4096], P(('grp', 'ch')), parts along dimension 0
- d_w_in: float32 [16384, 2048], P(('grp', 'ch')), parts along dimension 0
- d_w_out: float32 [16384, 2048], P(('grp', 'ch')), parts along dimension 0
- d_head: float32 [2048, 300], P('ch', 'grp'), parts along dimension 1
- mean_loss: float32 [2], P('grp'), parts along dimension 0
There are 2 independent parts, one for each index of `grp`. A program takes and returns all parts, laid end to end along the dimension named above; an argument that names none is the same for every part. Nothing has to cross between parts.
All inputs are finite; a program needn't handle non-finite values.
Results may differ from a plain program's by a relative error of at most 0.012.
Values may be sent and summed in bfloat16 or wider, within the bound.
A program may use at most 128 MiB of HBM per device.

v0:
```python
import jax
import jax.numpy as jnp
from jax import lax
from jax.sharding import PartitionSpec as P

KS = 7
WIN_H = 32
WIN_W = 32


norm_eps = 1e-06


def conv_apply(in_grid, kernel):
    half = KS // 2
    padded = jnp.pad(in_grid, ((0, 0), (half, half), (half, half)))
    running = jnp.zeros(in_grid.shape, in_grid.dtype)
    for row_shift in range(KS):
        for col_shift in range(KS):
            tap = kernel[:, row_shift * KS + col_shift]
            running = (
                running
                + tap[:, None, None]
                * padded[:, row_shift : row_shift + WIN_H, col_shift : col_shift + WIN_W]
            )
    return running


def gelu_parts(values):
    cum_prob = 0.5 * (1.0 + lax.erf(values * 0.7071067811865476))
    density = jnp.exp(-0.5 * values * values) * 0.3989422804014327
    return (values * cum_prob, cum_prob + values * density)


def per_device(features, dw_weight, norm_gain, layer_scale, w_in, w_out, w_head, labels):
    highest = lax.Precision.HIGHEST
    my_rows = features.shape[0]
    tok_count = features.shape[1]
    class_count = w_head.shape[1]
    row_offset = lax.axis_index("ch") * my_rows
    inputs_wide = features.astype(jnp.float32)
    in_grid = inputs_wide.reshape(my_rows, WIN_H, WIN_W)
    conv_out = conv_apply(in_grid, dw_weight).reshape(my_rows, tok_count).astype(jnp.bfloat16)
    conv_all = lax.all_gather(conv_out, "ch", axis=0, tiled=True)
    conv_wide = conv_all.astype(jnp.float32)
    tok_mean = jnp.mean(conv_wide, axis=0)
    centered = conv_wide - tok_mean[None, :]
    tok_var = jnp.mean(centered * centered, axis=0)
    inv_std = 1.0 / jnp.sqrt(tok_var + norm_eps)
    normed = centered * inv_std[None, :]
    norm_out = (norm_gain[:, None] * normed).astype(jnp.bfloat16)
    pre_act = jnp.dot(w_in, norm_out, preferred_element_type=jnp.float32)
    gelu_out, gelu_slope = gelu_parts(pre_act)
    hidden = gelu_out.astype(jnp.bfloat16)
    my_scale = lax.dynamic_slice_in_dim(layer_scale, row_offset, my_rows, 0)
    head_wide = w_head.astype(jnp.float32)
    my_head = lax.dynamic_slice_in_dim(head_wide, row_offset, my_rows, 0)
    w_cols = w_out
    branch_sum = lax.psum_scatter(
        lax.dot_general(
            w_cols, hidden, (((0,), (0,)), ((), ())), preferred_element_type=jnp.float32
        ),
        "ch",
        scatter_dimension=0,
        tiled=True,
    )
    block_out = inputs_wide + my_scale[:, None] * branch_sum
    part_logits = lax.dot_general(block_out, my_head, (((0,), (0,)), ((), ())), precision=highest)
    logits = lax.psum(part_logits, "ch")
    row_max = jnp.max(logits, axis=1, keepdims=True)
    exp_terms = jnp.exp(logits - row_max)
    exp_total = jnp.sum(exp_terms, axis=1, keepdims=True)
    log_total = jnp.log(exp_total) + row_max
    onehot = (labels[:, None] == jnp.arange(class_count, dtype=jnp.int32)[None, :]).astype(
        jnp.float32
    )
    picked = jnp.sum(logits * onehot, axis=1)
    mean_loss = jnp.mean(log_total[:, 0] - picked).reshape(1)
    logit_grad = exp_terms / exp_total - onehot
    out_grad = lax.dot_general(my_head, logit_grad, (((1,), (1,)), ((), ())), precision=highest)
    d_head = jnp.dot(block_out, logit_grad, precision=highest)
    d_scale = jnp.sum(out_grad * branch_sum, axis=1)
    branch_grad = (my_scale[:, None] * out_grad).astype(jnp.bfloat16)
    incoming = lax.all_gather(branch_grad, "ch", axis=0, tiled=True)
    w_cols = w_out
    hidden_acc = jnp.dot(w_cols, incoming, preferred_element_type=jnp.float32)
    tile_grad = lax.dot_general(
        hidden, incoming, (((1,), (1,)), ((), ())), preferred_element_type=jnp.float32
    )
    pre_grad = (hidden_acc * gelu_slope).astype(jnp.bfloat16)
    d_w_in = lax.dot_general(
        pre_grad, norm_out, (((1,), (1,)), ((), ())), preferred_element_type=jnp.float32
    )
    norm_grad = lax.dot_general(
        w_in, pre_grad, (((0,), (0,)), ((), ())), preferred_element_type=jnp.float32
    )
    gained = norm_gain[:, None] * norm_grad
    conv_term = (
        gained
        - jnp.mean(gained, axis=0)[None, :]
        - normed * jnp.mean(gained * normed, axis=0)[None, :]
    ) * inv_std[None, :]
    conv_grad = lax.psum_scatter(conv_term, "ch", scatter_dimension=0, tiled=True)
    unused, pullback = jax.vjp(conv_apply, in_grid, dw_weight)
    grid_grad, d_dw = pullback(conv_grad.reshape(my_rows, WIN_H, WIN_W))
    d_features = out_grad + grid_grad.reshape(my_rows, tok_count)
    return (d_features, d_dw, d_scale, d_w_in, tile_grad, d_head, mean_loss)


def solution(mesh):
    placed = (P("ch", "grp"), P("ch", None), P(), P(), P("ch", None), P("ch", None), P(), P("grp"))
    return jax.shard_map(
        per_device,
        mesh=mesh,
        in_specs=placed,
        out_specs=(
            P("ch", "grp"),
            P("ch", "grp"),
            P(("grp", "ch")),
            P(("grp", "ch"), None),
            P(("grp", "ch"), None),
            P("ch", "grp"),
            P("grp"),
        ),
        check_vma=False,
    )
```

profile of v0, /device:TPU:0, one launch (start us, length us, event | category | flops | bytes accessed | tf_op | source)
XLA Modules:
  0.0 497.7 jit_solution(14007070145774544614)
XLA Ops:
  10.4 1.1 copy.19
  11.6 4.8 add_convert_fusion
  16.5 56.0 %all-gather.3.cloned.1.call-done = bf16[2048,1024]{0,1:T(8,128)(2,1)} async-done(((bf16[128,1024]{0,1:T(8,128)(2,1)}), bf16[2048,1024]{0,1:T(8,128)(2,1)}) %all-gather.3.cloned.1.call-update) | async-done | bytes 4194320 | tf_op jit(solution)/shard_map/all_gather | solution.py:44
  72.5 3.0 convert_reduce_fusion
  75.9 1.2 fusion.9
  77.3 1.6 fusion.5
  79.0 2.4 fusion.31
  81.4 1.3 copy-done.7
  82.7 5.6 %convolution_bitcast_fusion = f32[2048,1024]{0,1:T(8,128)} fusion(bf16[512,2048]{1,0:T(8,128)(2,1)S(1)} %copy-done.45, f32[1024,512]{1,0:T(8,128)S(1)} %fusion.31), kind=kOutput, calls=%fused_computation.62 | convolution fusion | flops 2150105088 | bytes 12582912 | tf_op jit(solution)/shard_map/dot_general | solution.py:60
  89.2 102.4 %reduce-scatter.3.cloned.1.call-done = f32[128,1024]{0,1:T(8,128)} async-done(((f32[2048,1024]{0,1:T(8,128)}), f32[128,1024]{0,1:T(8,128)}) %reduce-scatter.3.cloned.1.call-update) | async-done | bytes 524304 | tf_op jit(solution)/shard_map/reduce_scatter | solution.py:59
  191.5 2.6 fusion.22
  194.2 91.7 %all-reduce.101.cloned.1.call-done = f32[1024,150]{0,1:T(8,128)} async-done(((f32[1024,150]{0,1:T(8,128)}), f32[1024,150]{0,1:T(8,128)}) %all-reduce.101.cloned.1.call-update) | async-done | bytes 614416 | tf_op jit(solution)/shard_map/psum | solution.py:69
  285.9 1.1 reduce_max.9
  287.0 1.2 select_reduce_fusion
  288.2 1.7 fusion.23
  290.9 2.5 multiply_reduce_fusion.1
  293.7 53.5 %all-gather.5.cloned.1.call-done = bf16[2048,1024]{0,1:T(8,128)(2,1)} async-done(((bf16[128,1024]{0,1:T(8,128)(2,1)}), bf16[2048,1024]{0,1:T(8,128)(2,1)}) %all-gather.5.cloned.1.call-update) | async-done | bytes 4194320 | tf_op jit(solution)/shard_map/all_gather | solution.py:84
  347.2 6.5 %fusion.15 = bf16[512,1024]{0,1:T(8,128)(2,1)S(1)} fusion(f32[1024,512]{1,0:T(8,128)} %copy-done.7, bf16[2048,1024]{0,1:T(8,128)(2,1)} %all-gather.5.cloned.1.call-done, bf16[512,2048]{1,0:T(8,128)(2,1)} %param.13), kind=kOutput, calls=%fused_computation.69 | convolution fusion | flops 2152726528 | bytes 9437184 | tf_op jit(solution)/shard_map/dot_general | solution.py:86
  353.7 3.0 fusion.6
  357.3 5.4 %fusion.8 = f32[2048,1024]{0,1:T(8,128)} fusion(bf16[2048,1024]{0,1:T(8,128)(2,1)S(1)} %copy-done.3, f32[1024,2048]{1,0:T(8,128)S(1)} %get-tuple-element.158, f32[1024]{0:T(1024)S(1)} %get-tuple-element.159, f32[1024]{0:T(1024)S(1)} %get-tuple-element.160, f32[2048]{0:T(1024)S(1)} %copy-done.13, f32[1024]{0:T(1024)S(1)} %add_rsqrt_fusion, ...), kind=kLoop, calls=%fused_computation.10 | loop fusion | flops 16777216 | bytes 20996096 | tf_op jit(solution)/shard_map/mul | solution.py:98
  364.1 1.5 fusion.21
  365.6 7.4 %fusion.32 = f32[512,2048]{1,0:T(8,128)} fusion(bf16[512,1024]{0,1:T(8,128)(2,1)} %copy-done.10, bf16[2048,1024]{0,1:T(8,128)(2,1)} %copy-done.4), kind=kOutput, calls=%fused_computation.255 | convolution fusion | flops 2147483648 | bytes 9437184 | tf_op jit(solution)/shard_map/dot_general | solution.py:91
  372.9 4.5 fusion.28
  377.5 88.5 %reduce-scatter.5.cloned.1.call-done = f32[128,1024]{0,1:T(8,128)} async-done(((f32[2048,1024]{0,1:T(8,128)}), f32[128,1024]{0,1:T(8,128)}) %reduce-scatter.5.cloned.1.call-update) | async-done | bytes 524304 | tf_op jit(solution)/shard_map/reduce_scatter | solution.py:103
  465.9 2.9 broadcast_multiply_fusion.2
  470.0 2.4 broadcast_multiply_fusion
  472.4 6.0 %pad_add_fusion = f32[128,38,38]{0,2,1:T(8,128)S(1)} fusion(f32[128,32,32]{0,2,1:T(8,128)S(1)} %get-tuple-element.66, f32[128,32,32]{0,2,1:T(8,128)S(1)} %get-tuple-element.67, f32[128,32,32]{0,2,1:T(8,128)S(1)} %get-tuple-element.68, f32[128,32,32]{0,2,1:T(8,128)S(1)} %get-tuple-element.69, f32[128,32,32]{0,2,1:T(8,128)S(1)} %get-tuple-element.70, ...), kind=kLoop, calls=%fused_computation.76 | loop fusion | flops 7762944 | bytes 23283712 | tf_op jit(solution)/shard_map/transpose(jvp())/add_any | solution.py:24
  478.4 3.1 pad_add_fusion.1
  481.5 2.1 copy.21
  483.5 2.1 add.438
  486.4 1.4 multiply_reduce_fusion.49
  487.8 1.4 multiply_reduce_fusion.50
  (116 shorter events, 9.8 us)
Async XLA Ops:
  7.2 71.8 %copy-start = (bf16[512,2048]{1,0:T(8,128)(2,1)S(1)}, bf16[512,2048]{1,0:T(8,128)(2,1)}, u32[]{:S(2)}) copy-start(bf16[512,2048]{1,0:T(8,128)(2,1)} %param.12) | copy-start | bytes 6291460
  7.2 65.3 %all-gather.3.cloned.1.call-start = ((), (), s32[]{:S(2)}) async-start(), calls=%async_computation.2 | async-start | bytes 4456448 | tf_op jit(solution)/shard_map/all_gather | solution.py:44
  9.2 67.9 %copy-start.29 = (f32[128]{0:T(128)}, f32[128]{0:T(128)S(1)}, u32[]{:S(2)}) copy-start(f32[128]{0:T(128)S(1)} %get-tuple-element.110) | copy-start | bytes 1540
  9.2 67.9 %copy-start.30 = (f32[128]{0:T(128)}, f32[128]{0:T(128)S(1)}, u32[]{:S(2)}) copy-start(f32[128]{0:T(128)S(1)} %get-tuple-element.111) | copy-start | bytes 1540
  9.2 67.9 %copy-start.31 = (f32[128]{0:T(128)}, f32[128]{0:T(128)S(1)}, u32[]{:S(2)}) copy-start(f32[128]{0:T(128)S(1)} %get-tuple-element.112) | copy-start | bytes 1540
  9.2 67.9 %copy-start.32 = (f32[128]{0:T(128)}, f32[128]{0:T(128)S(1)}, u32[]{:S(2)}) copy-start(f32[128]{0:T(128)S(1)} %get-tuple-element.113) | copy-start | bytes 1540
  9.3 67.9 %copy-start.33 = (f32[128]{0:T(128)}, f32[128]{0:T(128)S(1)}, u32[]{:S(2)}) copy-start(f32[128]{0:T(128)S(1)} %get-tuple-element.114) | copy-start | bytes 1540
  9.3 67.9 %copy-start.34 = (f32[128]{0:T(128)}, f32[128]{0:T(128)S(1)}, u32[]{:S(2)}) copy-start(f32[128]{0:T(128)S(1)} %get-tuple-element.115) | copy-start | bytes 1540
  9.3 67.9 %copy-start.35 = (f32[128]{0:T(128)}, f32[128]{0:T(128)S(1)}, u32[]{:S(2)}) copy-start(f32[128]{0:T(128)S(1)} %get-tuple-element.116) | copy-start | bytes 1540
  9.3 67.9 %copy-start.36 = (f32[128]{0:T(128)}, f32[128]{0:T(128)S(1)}, u32[]{:S(2)}) copy-start(f32[128]{0:T(128)S(1)} %get-tuple-element.117) | copy-start | bytes 1540
  9.3 67.9 %copy-start.37 = (f32[128]{0:T(128)}, f32[128]{0:T(128)S(1)}, u32[]{:S(2)}) copy-start(f32[128]{0:T(128)S(1)} %get-tuple-element.118) | copy-start | bytes 1540
  9.3 67.9 %copy-start.38 = (f32[128]{0:T(128)}, f32[128]{0:T(128)S(1)}, u32[]{:S(2)}) copy-start(f32[128]{0:T(128)S(1)} %get-tuple-element.119) | copy-start | bytes 1540
  9.3 67.9 %copy-start.39 = (f32[128]{0:T(128)}, f32[128]{0:T(128)S(1)}, u32[]{:S(2)}) copy-start(f32[128]{0:T(128)S(1)} %get-tuple-element.120) | copy-start | bytes 1540
  9.3 67.9 %copy-start.40 = (f32[128]{0:T(128)}, f32[128]{0:T(128)S(1)}, u32[]{:S(2)}) copy-start(f32[128]{0:T(128)S(1)} %get-tuple-element.121) | copy-start | bytes 1540
  10.4 65.1 %copy-start.20 = (f32[128]{0:T(128)}, f32[128]{0:T(128)S(1)}, u32[]{:S(2)}) copy-start(f32[128]{0:T(128)S(1)} %get-tuple-element.136) | copy-start | bytes 1540
  10.4 65.1 %copy-start.22 = (f32[128]{0:T(128)}, f32[128]{0:T(128)S(1)}, u32[]{:S(2)}) copy-start(f32[128]{0:T(128)S(1)} %get-tuple-element.137) | copy-start | bytes 1540
  10.4 66.9 %copy-start.24 = (f32[128]{0:T(128)}, f32[128]{0:T(128)S(1)}, u32[]{:S(2)}) copy-start(f32[128]{0:T(128)S(1)} %get-tuple-element.138) | copy-start | bytes 1540
  10.4 66.9 %copy-start.26 = (f32[128]{0:T(128)}, f32[128]{0:T(128)S(1)}, u32[]{:S(2)}) copy-start(f32[128]{0:T(128)S(1)} %get-tuple-element.139) | copy-start | bytes 1540
  16.4 175.1 %reduce-scatter.3.cloned.1.call-start = ((), (), s32[]{:S(2)}) async-start(), calls=%async_computation.3 | async-start | bytes 8912896 | tf_op jit(solution)/shard_map/reduce_scatter | solution.py:59
  88.3 198.7 %copy-start.41 = (s32[1024]{0:T(1024)S(1)}, s32[1024]{0:T(1024)}, u32[]{:S(2)}) copy-start(s32[1024]{0:T(1024)} %param.15) | copy-start | bytes 12292
  88.4 197.5 %all-reduce.101.cloned.1.call-start = ((), (), s32[]{:S(2)}) async-start(), calls=%async_computation.4 | async-start | bytes 1245184 | tf_op jit(solution)/shard_map/psum | solution.py:69
  89.2 105.0 %copy-start.43 = (f32[128]{0:T(128)}, f32[128]{0:T(128)S(1)}, u32[]{:S(2)}) copy-start(f32[128]{0:T(128)S(1)} %dynamic_slice.7) | copy-start | bytes 1540
  194.1 153.1 %all-gather.5.cloned.1.call-start = ((), (), s32[]{:S(2)}) async-start(), calls=%async_computation.5 | async-start | bytes 4456448 | tf_op jit(solution)/shard_map/all_gather | solution.py:84
  289.9 63.7 %copy-start.11 = (f32[128,1024]{1,0:T(8,128)}, f32[128,1024]{1,0:T(8,128)S(1)}, u32[]{:S(2)}) copy-start(f32[128,1024]{1,0:T(8,128)S(1)} %fusion.23) | copy-start | bytes 1572868
  293.4 172.5 %reduce-scatter.5.cloned.1.call-start = ((), (), s32[]{:S(2)}) async-start(), calls=%async_computation.6 | async-start | bytes 8912896 | tf_op jit(solution)/shard_map/reduce_scatter | solution.py:103
  377.4 91.4 %copy-start.15 = (f32[128]{0:T(128)S(1)}, f32[128]{0:T(128)}, u32[]{:S(2)}) copy-start(f32[128]{0:T(128)} %copy-done.14) | copy-start | bytes 1540
  377.4 91.4 %copy-start.17 = (f32[128]{0:T(128)S(1)}, f32[128]{0:T(128)}, u32[]{:S(2)}) copy-start(f32[128]{0:T(128)} %copy-done.16) | copy-start | bytes 1540
  377.4 91.4 %copy-start.19 = (f32[128]{0:T(128)S(1)}, f32[128]{0:T(128)}, u32[]{:S(2)}) copy-start(f32[128]{0:T(128)} %copy-done.18) | copy-start | bytes 1540
  377.5 91.4 %copy-start.21 = (f32[128]{0:T(128)S(1)}, f32[128]{0:T(128)}, u32[]{:S(2)}) copy-start(f32[128]{0:T(128)} %copy-done.20) | copy-start | bytes 1540
  377.5 91.4 %copy-start.23 = (f32[128]{0:T(128)S(1)}, f32[128]{0:T(128)}, u32[]{:S(2)}) copy-start(f32[128]{0:T(128)} %copy-done.22) | copy-start | bytes 1540
  377.5 91.4 %copy-start.25 = (f32[128]{0:T(128)S(1)}, f32[128]{0:T(128)}, u32[]{:S(2)}) copy-start(f32[128]{0:T(128)} %copy-done.24) | copy-start | bytes 1540
  377.5 91.4 %copy-start.27 = (f32[128]{0:T(128)S(1)}, f32[128]{0:T(128)}, u32[]{:S(2)}) copy-start(f32[128]{0:T(128)} %copy-done.26) | copy-start | bytes 1540
  (19 other events, 197.3 us)
Sparse Core Ops, SparseCore 0:
  16.5 55.9 all-gather.2
  88.5 103.0 reduce-scatter.2
  195.5 90.2 all-reduce.100
  293.5 53.5 all-gather.4
  362.9 102.9 reduce-scatter.4
where the time goes:
time: 498 us
  waiting for transfers between devices  392 us (79%)
  other arithmetic  44 us (9%)
  matrix products  35 us (7%)
  between operations  16.2 us (3%)
  local copies, waits for them, and re-layouts  9.9 us (2%)
    reduce_scatter x1, waiting for transfers between devices, per_device(): lax.psum_scatter(lax.dot_general(w_cols, hidden, (((0,), (0,)), ((), ()))...  102 us
    psum x1, waiting for transfers between devices, per_device(): logits = lax.psum(part_logits, 'ch')  91.7 us
    reduce_scatter x1, waiting for transfers between devices, per_device(): lax.psum_scatter(conv_term, 'ch', scatter_dimension=0, tiled=True)  88.5 us
    all_gather x1, waiting for transfers between devices, per_device(): conv_all = lax.all_gather(conv_out, 'ch', axis=0, tiled=True)  56 us
    all_gather x1, waiting for transfers between devices, per_device(): incoming = lax.all_gather(branch_grad, 'ch', axis=0, tiled=True)  53.5 us
  transfers between devices with their start and end apart: 5, of which 5 were waited for; matrix products, arithmetic and copies ran while one was open for 3% of the time, Pallas kernels for 0%

commit v1 on v0

v1 whole, which is shorter than its diff:
```python
import functools
import jax
import jax.numpy as jnp
from jax import lax
from jax.experimental import pallas as pl
from jax.experimental.pallas import tpu as pltpu
from jax.sharding import PartitionSpec as P

KS = 7
WIN_H = 32
WIN_W = 32

norm_eps = 1e-06
VMEM_LIMIT = 56 * 1024 * 1024


def conv_apply(in_grid, kernel):
    half = KS // 2
    padded = jnp.pad(in_grid, ((0, 0), (half, half), (half, half)))
    running = jnp.zeros(in_grid.shape, in_grid.dtype)
    for row_shift in range(KS):
        for col_shift in range(KS):
            tap = kernel[:, row_shift * KS + col_shift]
            running = (
                running
                + tap[:, None, None]
                * padded[:, row_shift : row_shift + WIN_H, col_shift : col_shift + WIN_W]
            )
    return running


def gelu_parts(values):
    cum_prob = 0.5 * (1.0 + lax.erf(values * 0.7071067811865476))
    density = jnp.exp(-0.5 * values * values) * 0.3989422804014327
    return (values * cum_prob, cum_prob + values * density)


def place(n):
    me = lax.axis_index("ch")
    return lax.div(me, 4), lax.rem(lax.div(me, 2), 2), lax.rem(me, 2)


def index_of(z, y, c):
    return (z * 2 + y) * 2 + c


def greet(devices, z, a):
    barrier = pltpu.get_barrier_semaphore()
    for device in devices:
        pl.semaphore_signal(barrier, inc=1, device_id={"ch": device})
    me = lax.axis_index("ch")

    @pl.when(z > 0)
    def _():
        pl.semaphore_signal(barrier, inc=1, device_id={"ch": me - 4})

    @pl.when(z < a - 1)
    def _():
        pl.semaphore_signal(barrier, inc=1, device_id={"ch": me + 4})

    count = len(devices) + jnp.where(z > 0, 1, 0) + jnp.where(z < a - 1, 1, 0)
    pl.semaphore_wait(barrier, count)


def gather_kernel(n, x_ref, out_ref, send_sem, recv_sem):
    a = n // 4
    rows = x_ref.shape[0]
    z, y, c = place(n)
    me = index_of(z, y, c)
    twin, across = index_of(z, y, 1 - c), index_of(z, 1 - y, c)
    greet([twin, across], z, a)

    def block(b):
        return out_ref.at[pl.ds(pl.multiple_of(b * rows, rows), rows)]

    def copy(kind, b, device):
        return pltpu.make_async_remote_copy(
            src_ref=block(b),
            dst_ref=block(b),
            send_sem=send_sem.at[kind, b],
            recv_sem=recv_sem.at[b],
            device_id={"ch": device},
        )

    out_ref[pl.ds(pl.multiple_of(me * rows, rows), rows)] = x_ref[...]

    @pl.when(z < a - 1)
    def _():
        copy(0, me, me + 4).start()

    @pl.when(z > 0)
    def _():
        copy(1, me, me - 4).start()

    copy(2, me, across).start()
    copy(3, me, twin).start()

    def from_line(s):
        below, above = me - 4 * s, me + 4 * s

        @pl.when(z >= s)
        def _():
            copy(0, below, me).wait_recv()

            @pl.when(z < a - 1)
            def _():
                copy(0, below, me + 4).start()

            copy(2, below, across).start()
            copy(3, below, twin).start()

        @pl.when(z + s < a)
        def _():
            copy(1, above, me).wait_recv()

            @pl.when(z > 0)
            def _():
                copy(1, above, me - 4).start()

            copy(2, above, across).start()
            copy(3, above, twin).start()

    def from_across(s):
        def take(b):
            copy(2, b, across).wait_recv()
            copy(3, b, twin).start()

        if s == 0:
            take(across)
            return

        @pl.when(z >= s)
        def _():
            take(across - 4 * s)

        @pl.when(z + s < a)
        def _():
            take(across + 4 * s)

    for s in range(1, a):
        from_line(s)
        from_across(s - 1)
    from_across(a - 1)

    for q in range(n // 2):
        copy(3, q * 2 + 1 - c, twin).wait_recv()
        copy(3, q * 2 + c, twin).wait_send()
    for zz in range(a):
        copy(2, index_of(zz, y, c), across).wait_send()

        @pl.when((z < a - 1) & (zz <= z))
        def _():
            copy(0, index_of(zz, y, c), me + 4).wait_send()

        @pl.when((z > 0) & (zz >= z))
        def _():
            copy(1, index_of(zz, y, c), me - 4).wait_send()


def gather(n, x):
    rows, cols = x.shape
    return pl.pallas_call(
        functools.partial(gather_kernel, n),
        out_shape=jax.ShapeDtypeStruct((n * rows, cols), x.dtype),
        in_specs=[pl.BlockSpec(memory_space=pltpu.VMEM)],
        out_specs=pl.BlockSpec(memory_space=pltpu.VMEM),
        scratch_shapes=[pltpu.SemaphoreType.DMA((4, n)), pltpu.SemaphoreType.DMA((n,))],
        compiler_params=pltpu.CompilerParams(
            collective_id=0, has_side_effects=True, vmem_limit_bytes=VMEM_LIMIT
        ),
    )(x)


def total_kernel(n, x_ref, out_ref, buf, from_twin, acc, slots, sums, t_sem, r_sem, g_sem, f_sem):
    m = n // 2
    height, cols = x_ref.shape
    strips = cols // 128
    half = height * strips // 2
    rows = half // m
    me = lax.axis_index("ch")
    q, c = lax.div(me, 2), lax.rem(me, 2)
    twin = q * 2 + 1 - c
    barrier = pltpu.get_barrier_semaphore()
    pl.semaphore_signal(barrier, inc=1, device_id={"ch": twin})
    for d in range(1, m):
        pl.semaphore_signal(barrier, inc=1, device_id={"ch": lax.rem(q + d, m) * 2 + c})
    for j in range(strips):
        buf[j * height : (j + 1) * height, :] = x_ref[:, j * 128 : (j + 1) * 128]
    pl.semaphore_wait(barrier, m)

    def piece(ref, start, length):
        return ref.at[pl.ds(pl.multiple_of(start, 8), length)]

    swap = pltpu.make_async_remote_copy(
        src_ref=piece(buf, (1 - c) * half, half),
        dst_ref=from_twin,
        send_sem=t_sem.at[0],
        recv_sem=t_sem.at[1],
        device_id={"ch": twin},
    )
    swap.start()
    swap.wait_recv()
    acc[...] = buf[pl.ds(pl.multiple_of(c * half, 8), half), :] + from_twin[...]

    def scatter(d):
        other = lax.rem(q + d, m)
        return pltpu.make_async_remote_copy(
            src_ref=piece(acc, other * rows, rows),
            dst_ref=slots.at[d],
            send_sem=r_sem.at[0, d],
            recv_sem=r_sem.at[1, d],
            device_id={"ch": other * 2 + c},
        )

    for d in range(1, m):
        scatter(d).start()
    mine = acc[pl.ds(pl.multiple_of(q * rows, 8), rows), :]
    for d in range(1, m):
        scatter(d).wait_recv()
        mine = mine + slots[d]
    my_start = c * half + q * rows
    sums[pl.ds(pl.multiple_of(my_start, 8), rows), :] = mine

    def spread(d, start, device):
        return pltpu.make_async_remote_copy(
            src_ref=piece(sums, start, rows),
            dst_ref=piece(sums, start, rows),
            send_sem=g_sem.at[0, d],
            recv_sem=g_sem.at[1, d],
            device_id={"ch": device},
        )

    def forward(d, start):
        return pltpu.make_async_remote_copy(
            src_ref=piece(sums, start, rows),
            dst_ref=piece(sums, start, rows),
            send_sem=f_sem.at[0, d],
            recv_sem=f_sem.at[1, d],
            device_id={"ch": twin},
        )

    for d in range(1, m):
        spread(d, my_start, lax.rem(q + d, m) * 2 + c).start()
    forward(0, my_start).start()
    for d in range(1, m):
        start = c * half + lax.rem(q - d + m, m) * rows
        spread(d, start, twin).wait_recv()
        forward(d, start).start()
    for d in range(m):
        forward(d, (1 - c) * half + lax.rem(q - d + m, m) * rows).wait_recv()
    for j in range(strips):
        out_ref[:, j * 128 : (j + 1) * 128] = sums[j * height : (j + 1) * height, :]
    swap.wait_send()
    for d in range(1, m):
        scatter(d).wait_send()
        spread(d, my_start, twin).wait_send()
    for d in range(m):
        forward(d, my_start).wait_send()


def total(n, x):
    height, cols = x.shape
    area = height * (cols // 128)
    m = n // 2
    return pl.pallas_call(
        functools.partial(total_kernel, n),
        out_shape=jax.ShapeDtypeStruct(x.shape, x.dtype),
        in_specs=[pl.BlockSpec(memory_space=pltpu.VMEM)],
        out_specs=pl.BlockSpec(memory_space=pltpu.VMEM),
        scratch_shapes=[
            pltpu.VMEM((area, 128), jnp.float32),
            pltpu.VMEM((area // 2, 128), jnp.float32),
            pltpu.VMEM((area // 2, 128), jnp.float32),
            pltpu.VMEM((m, area // n, 128), jnp.float32),
            pltpu.VMEM((area, 128), jnp.float32),
            pltpu.SemaphoreType.DMA((2,)),
            pltpu.SemaphoreType.DMA((2, m)),
            pltpu.SemaphoreType.DMA((2, m)),
            pltpu.SemaphoreType.DMA((2, m)),
        ],
        compiler_params=pltpu.CompilerParams(
            collective_id=1, has_side_effects=True, vmem_limit_bytes=VMEM_LIMIT
        ),
    )(x)


def scatter_kernel(
    n, g_ref, out_ref, t_in, y_in, u_in, d_in, y_out, z_out, t_sem, y_sem, u_sem, d_sem, zs_sem
):
    a = n // 4
    rows = out_ref.shape[0]
    z, y, c = place(n)
    me = index_of(z, y, c)
    twin, across = index_of(z, y, 1 - c), index_of(z, 1 - y, c)
    greet([twin, across], z, a)

    def own(b):
        return pl.ds(pl.multiple_of(b * rows, rows), rows)

    def order(k):
        if k == a - 1:
            return z
        low = jnp.where(k < a - 1 - z, a - 1 - k, k - (a - 1 - z))
        high = jnp.where(k < z, k, a - 1 - (k - z))
        return jnp.where(2 * z < a, low, high)

    def to_twin(zz, side, core):
        return pltpu.make_async_remote_copy(
            src_ref=g_ref.at[own(index_of(zz, side, core))],
            dst_ref=t_in.at[zz * 2 + side],
            send_sem=t_sem.at[0, zz * 2 + side],
            recv_sem=t_sem.at[1, zz * 2 + side],
            device_id={"ch": twin},
        )

    def to_across(k, zz):
        return pltpu.make_async_remote_copy(
            src_ref=y_out.at[k],
            dst_ref=y_in.at[zz],
            send_sem=y_sem.at[0, zz],
            recv_sem=y_sem.at[1, zz],
            device_id={"ch": across},
        )

    def along(k, zz, landing, sem, device):
        return pltpu.make_async_remote_copy(
            src_ref=z_out.at[k],
            dst_ref=landing.at[zz],
            send_sem=zs_sem.at[k],
            recv_sem=sem.at[zz],
            device_id={"ch": device},
        )

    for k in range(a):
        to_twin(order(k), 1 - y, 1 - c).start()
    for k in range(a):
        to_twin(order(k), y, 1 - c).start()
    for k in range(a):
        zz = order(k)
        to_twin(zz, 1 - y, c).wait_recv()
        y_out[k] = (
            g_ref[own(index_of(zz, 1 - y, c))].astype(jnp.float32)
            + t_in[zz * 2 + 1 - y].astype(jnp.float32)
        ).astype(jnp.bfloat16)
        to_across(k, zz).start()
    for k in range(a):
        zz = order(k)
        to_twin(zz, y, c).wait_recv()
        to_across(k, zz).wait_recv()
        term = (
            g_ref[own(index_of(zz, y, c))].astype(jnp.float32)
            + t_in[zz * 2 + y].astype(jnp.float32)
            + y_in[zz].astype(jnp.float32)
        )
        if k < a - 1:
            out_ref[...] = term

            @pl.when((zz > z) & (z > 0))
            def _():
                along(k, zz, u_in, u_sem, me).wait_recv()
                out_ref[...] += u_in[zz].astype(jnp.float32)

            @pl.when((zz < z) & (z < a - 1))
            def _():
                along(k, zz, d_in, d_sem, me).wait_recv()
                out_ref[...] += d_in[zz].astype(jnp.float32)

            z_out[k] = out_ref[...].astype(jnp.bfloat16)

            @pl.when(zz > z)
            def _():
                along(k, zz, u_in, u_sem, me + 4).start()

            @pl.when(zz < z)
            def _():
                along(k, zz, d_in, d_sem, me - 4).start()

        else:
            out_ref[...] = term

            @pl.when(z > 0)
            def _():
                along(0, z, u_in, u_sem, me).wait_recv()
                out_ref[...] += u_in[z].astype(jnp.float32)

            @pl.when(z < a - 1)
            def _():
                along(0, z, d_in, d_sem, me).wait_recv()
                out_ref[...] += d_in[z].astype(jnp.float32)

    for k in range(a):
        zz = order(k)
        to_twin(zz, 1 - y, 1 - c).wait_send()
        to_twin(zz, y, 1 - c).wait_send()
        to_across(k, zz).wait_send()
        if k < a - 1:
            along(k, zz, u_in, u_sem, me).wait_send()


def scatter(n, g):
    rows, cols = g.shape[0] // n, g.shape[1]
    a = n // 4
    return pl.pallas_call(
        functools.partial(scatter_kernel, n),
        out_shape=jax.ShapeDtypeStruct((rows, cols), jnp.float32),
        in_specs=[pl.BlockSpec(memory_space=pltpu.VMEM)],
        out_specs=pl.BlockSpec(memory_space=pltpu.VMEM),
        scratch_shapes=[
            pltpu.VMEM((n // 2, rows, cols), jnp.bfloat16),
            pltpu.VMEM((a, rows, cols), jnp.bfloat16),
            pltpu.VMEM((a, rows, cols), jnp.bfloat16),
            pltpu.VMEM((a, rows, cols), jnp.bfloat16),
            pltpu.VMEM((a, rows, cols), jnp.bfloat16),
            pltpu.VMEM((a, rows, cols), jnp.bfloat16),
            pltpu.SemaphoreType.DMA((2, n // 2)),
            pltpu.SemaphoreType.DMA((2, a)),
            pltpu.SemaphoreType.DMA((a,)),
            pltpu.SemaphoreType.DMA((a,)),
            pltpu.SemaphoreType.DMA((a,)),
        ],
        compiler_params=pltpu.CompilerParams(
            collective_id=2, has_side_effects=True, vmem_limit_bytes=VMEM_LIMIT
        ),
    )(g)


def dot(lhs, rhs, over, precision=None):
    return lax.dot_general(
        lhs, rhs, ((over[:1], over[1:]), ((), ())),
        precision=precision, preferred_element_type=jnp.float32,
    )


def per_device(n, features, dw_weight, norm_gain, layer_scale, w_in, w_out, w_head, labels):
    fine = lax.Precision.HIGH
    my_rows, tok_count = features.shape
    channels, class_count = w_head.shape
    row_offset = lax.axis_index("ch") * my_rows
    inputs_wide = features.astype(jnp.float32)
    in_grid = inputs_wide.reshape(my_rows, WIN_H, WIN_W)
    conv_out = conv_apply(in_grid, dw_weight).reshape(my_rows, tok_count).astype(jnp.bfloat16)
    conv_all = gather(n, conv_out)
    conv_wide = conv_all.astype(jnp.float32)
    tok_mean = jnp.mean(conv_wide, axis=0)
    centered = conv_wide - tok_mean[None, :]
    tok_var = jnp.mean(centered * centered, axis=0)
    inv_std = 1.0 / jnp.sqrt(tok_var + norm_eps)
    norm_out = (norm_gain[:, None] * (centered * inv_std[None, :])).astype(jnp.bfloat16)
    pre_act = jnp.dot(w_in, norm_out, preferred_element_type=jnp.float32)
    gelu_out, gelu_slope = gelu_parts(pre_act)
    hidden = gelu_out.astype(jnp.bfloat16)

    classes = -(-class_count // max(n, 16)) * max(n, 16)
    head_pad = jnp.pad(w_head, ((0, 0), (0, classes - class_count)))
    head_wide = head_pad.astype(jnp.float32)
    my_scale = lax.dynamic_slice_in_dim(layer_scale, row_offset, my_rows, 0)
    my_head = lax.dynamic_slice_in_dim(head_pad, row_offset, my_rows, 0)
    my_head_wide = my_head.astype(jnp.float32)
    scaled_head = layer_scale[:, None] * head_wide
    mixed = dot(w_out.astype(jnp.float32), scaled_head, (1, 0), fine)
    part = dot(mixed, hidden.astype(jnp.float32), (0, 0), fine) + dot(my_head, features, (0, 0))
    logits = total(n, part)

    kinds = lax.broadcasted_iota(jnp.int32, (classes, tok_count), 0)
    logits = jnp.where(kinds < class_count, logits, -jnp.inf)
    row_max = jnp.max(logits, axis=0, keepdims=True)
    exp_terms = jnp.exp(logits - row_max)
    exp_total = jnp.sum(exp_terms, axis=0, keepdims=True)
    log_total = jnp.log(exp_total) + row_max
    hit = kinds == labels[None, :]
    picked = jnp.sum(jnp.where(hit, logits, 0.0), axis=0)
    mean_loss = jnp.mean(log_total[0] - picked).reshape(1)
    logit_grad = exp_terms / exp_total - hit.astype(jnp.float32)
    grad_narrow = logit_grad.astype(jnp.bfloat16)

    out_grad = dot(my_head_wide, logit_grad, (1, 0), fine)
    seen = dot(hidden, grad_narrow, (1, 1))
    hidden_grad = dot(mixed, logit_grad, (1, 0), fine)
    seen_narrow = seen.astype(jnp.bfloat16)
    d_w_out = dot(seen_narrow, scaled_head.astype(jnp.bfloat16), (1, 1))
    branch_seen = dot(w_out, seen_narrow, (0, 0)).astype(jnp.bfloat16)
    pre_grad_wide = hidden_grad * gelu_slope
    pre_grad = pre_grad_wide.astype(jnp.bfloat16)
    d_w_in = dot(pre_grad, norm_out, (1, 1))
    gain_rows = jnp.sum(w_in.astype(jnp.float32) * norm_gain[None, :], axis=1)
    mean_gained = jnp.sum(gain_rows[:, None] * pre_grad_wide, axis=0) / channels
    mean_both = jnp.sum(pre_act * pre_grad_wide, axis=0) / channels
    norm_grad = dot(w_in, pre_grad, (0, 0))
    conv_term = (
        norm_gain[:, None] * norm_grad
        - mean_gained[None, :]
        - (centered * inv_std[None, :]) * mean_both[None, :]
    ) * inv_std[None, :]
    width = -(-classes // 128) * 128
    payload = jnp.concatenate(
        [
            conv_term.astype(jnp.bfloat16),
            jnp.pad(branch_seen, ((0, 0), (0, width - classes))),
        ],
        axis=1,
    )
    landed = scatter(n, payload)
    conv_grad = landed[:, :tok_count]
    my_seen = landed[:, tok_count : tok_count + class_count]
    d_head = dot(inputs_wide, logit_grad, (1, 1), fine)[:, :class_count] + my_scale[:, None] * my_seen
    d_scale = jnp.sum(my_head_wide[:, :class_count] * my_seen, axis=1)
    unused, pullback = jax.vjp(conv_apply, in_grid, dw_weight)
    grid_grad, d_dw = pullback(conv_grad.reshape(my_rows, WIN_H, WIN_W))
    d_features = out_grad + grid_grad.reshape(my_rows, tok_count)
    return (d_features, d_dw, d_scale, d_w_in, d_w_out, d_head, mean_loss)


def solution(mesh):
    placed = (P("ch", "grp"), P("ch", None), P(), P(), P("ch", None), P("ch", None), P(), P("grp"))
    return jax.shard_map(
        functools.partial(per_device, mesh.shape["ch"]),
        mesh=mesh,
        in_specs=placed,
        out_specs=(
            P("ch", "grp"),
            P("ch", "grp"),
            P(("grp", "ch")),
            P(("grp", "ch"), None),
            P(("grp", "ch"), None),
            P("ch", "grp"),
            P("grp"),
        ),
        check_vma=False,
    )
```

time: 498 us -> 188 us (0.38)
  waiting for transfers between devices: 392 us -> 0 us
  Pallas kernels: 0 us -> 100 us
  between operations: 16.2 us -> 4.17 us
  other arithmetic: 44 us -> 37.1 us
    reduce_scatter x2 -> x0, waiting for transfers between devices: 191 us -> none  [the longest x1 102 us: per_device(): lax.psum_scatter(lax.dot_general(w_cols, hidden, (((0,), (0,)), ((), ()))...]
    all_gather x2 -> x0, waiting for transfers between devices: 110 us -> none  [the longest x1 56 us: per_device(): conv_all = lax.all_gather(conv_out, 'ch', axis=0, tiled=True)]
    pallas_call x0 -> x3, Pallas kernels: none -> 100 us  [the longest x1 41.7 us: scatter(): pl.pallas_call(functools.partial(scatter_kernel, n), out_shape=jax.ShapeD...]
    psum x1 -> x0, waiting for transfers between devices: 91.7 us -> none  [per_device(): logits = lax.psum(part_logits, 'ch')]
    mul x1 -> x0, other arithmetic: 5.42 us -> none  [per_device(): (gained - jnp.mean(gained, axis=0)[None, :] - normed * jnp.mean(gained *...]
    concatenate x0 -> x1, other arithmetic: none -> 5.11 us  [per_device(): jnp.concatenate([conv_term.astype(jnp.bfloat16), jnp.pad(branch_seen, ((0...]
    dot_general x8 -> x11, matrix products: 32.6 us -> 29.3 us  [dot(): lax.dot_general(lhs, rhs, ((over[:1], over[1:]), ((), ())), precision=pre...]
  transfers between devices with their start and end apart: 5 -> 0, of which waited for: 5 -> 0; matrix products, arithmetic and copies ran while one was open for 3% -> 0% of each run, Pallas kernels for 0% -> 0%
where the time goes in v1:
time: 188 us; the launch traced here: 187 us
  Pallas kernels  100 us (53%)
  other arithmetic  37.1 us (20%)
  matrix products  33.4 us (18%)
  local copies, waits for them, and re-layouts  12.4 us (7%)
  between operations  4.17 us (2%)
    pallas_call x1, Pallas kernels, scatter(): pl.pallas_call(functools.partial(scatter_kernel, n), out_shape=jax.ShapeD...  41.7 us
    pallas_call x1, Pallas kernels, gather(): pl.pallas_call(functools.partial(gather_kernel, n), out_shape=jax.ShapeDt...  35.5 us
    dot_general x11, matrix products, dot(): lax.dot_general(lhs, rhs, ((over[:1], over[1:]), ((), ())), precision=pre...  29.3 us
    pallas_call x1, Pallas kernels, total(): pl.pallas_call(functools.partial(total_kernel, n), out_shape=jax.ShapeDty...  22.9 us
    add_any x2, other arithmetic, conv_apply(): padded[:, row_shift:row_shift + WIN_H, col_shift:col_shift + WIN_W]  6.8 us
    mul x3, other arithmetic, conv_apply(): tap[:, None, None]  5.48 us
    concatenate x1, other arithmetic, per_device(): jnp.concatenate([conv_term.astype(jnp.bfloat16), jnp.pad(branch_seen, ((0...  5.11 us
    convert_element_type x1, other arithmetic, per_device(): conv_apply(in_grid, dw_weight).reshape(my_rows, tok_count)  4.81 us

profile of v1, /device:TPU:0, one launch (start us, length us, event | category | flops | bytes accessed | tf_op | source)
XLA Modules:
  0.0 187.2 jit_solution(14999987568094485137)
XLA Ops:
  1.9 1.6 slice_bitcast_fusion.47
  3.5 1.4 slice_bitcast_fusion.46
  6.1 4.8 %add_convert_fusion = bf16[128,32,32]{0,2,1:T(8,128)(2,1)S(1)} fusion(f32[128,32,32]{0,2,1:T(8,128)S(1)} %bitcast.241, f32[128]{0:T(128)S(1)} %get-tuple-element.180, f32[128]{0:T(128)} %get-tuple-element.181, f32[128]{0:T(128)S(1)} %get-tuple-element.134, f32[128]{0:T(128)S(1)} %get-tuple-element.135, f32[128]{0:T(128)S(1)} %get-tuple-element.136, ...), kind=kLoop, calls=%fused_computation.159 | loop fusion | flops 12845056 | bytes 811520 | tf_op jit(solution)/shard_map/convert_element_type | solution.py:441
  11.8 35.5 %shard_map.135 = bf16[2048,1024]{1,0:T(8,128)(2,1)} custom-call(bf16[128,1024]{1,0:T(8,128)(2,1)} %copy.31.x_ref), custom_call_target="tpu_custom_call" | custom-call | tf_op jit(solution)/shard_map/pallas_call | solution.py:162
  47.3 3.0 %convert_reduce_fusion = f32[1024]{0:T(1024)S(1)} fusion(bf16[2048,1024]{1,0:T(8,128)(2,1)} %shard_map.135), kind=kLoop, calls=%fused_computation.1 | loop fusion | flops 4193280 | bytes 4198400 | tf_op jit(solution)/shard_map/reduce_sum | solution.py:444
  50.8 1.1 fusion.9
  52.0 4.2 %fusion.19 = (bf16[512,1024]{1,0:T(8,128)(2,1)}, f32[1024,512]{0,1:T(8,128)}) fusion(bf16[512,2048]{1,0:T(8,128)(2,1)S(1)} %copy-done.9, bf16[2048,1024]{1,0:T(8,128)(2,1)S(1)} %copy-done.2, f32[1024]{0:T(1024)S(1)} %add_rsqrt_fusion, f32[1024]{0:T(1024)S(1)} %broadcast_multiply_fusion.51, f32[2048]{0:T(1024)S(1)} %copy-done.23), kind=kOutput, calls=%fused_computation.76 | convolution fusion | flops 2160590848 | bytes 9453568 | tf_op jit(solution)/shard_map/dot_general | solution.py:449
  56.2 1.6 copy.29
  57.8 2.7 %fusion.22 = f32[160,512]{1,0:T(8,128)S(1)} fusion(bf16[512,2048]{1,0:T(8,128)(2,1)S(1)} %copy-done, f32[2048]{0:T(1024)S(1)} %copy-done.17, bf16[2048,150]{1,0:T(8,128)(2,1)S(1)} %copy.29), kind=kOutput, calls=%fused_computation.81 | convolution fusion | flops 1007288320 | bytes 3047424 | tf_op jit(solution)/shard_map/dot_general | solution.py:428
  61.2 1.3 fusion.39
  62.5 2.3 %convolution_add_fusion.x_ref = f32[160,1024]{1,0:T(8,128)} fusion(f32[160,1024]{1,0:T(8,128)} %fusion.39, bf16[128,1024]{1,0:T(8,128)(2,1)S(1)} %copy-done.8, s32[]{:T(128)S(6)} %select_n.11, bf16[2048,150]{1,0:T(8,128)(2,1)S(1)} %copy.29), kind=kOutput, calls=%fused_computation.82 | convolution fusion | flops 42106880 | bytes 2187268 | tf_op jit(solution)/shard_map/dot_general | solution.py:428
  64.9 22.9 %shard_map.136 = f32[160,1024]{1,0:T(8,128)} custom-call(f32[160,1024]{1,0:T(8,128)} %convolution_add_fusion.x_ref), custom_call_target="tpu_custom_call" | custom-call | tf_op jit(solution)/shard_map/pallas_call | solution.py:265
  87.8 1.4 select_reduce_fusion.1
  89.2 1.3 select_reduce_fusion
  90.5 1.6 convolution_bitcast_fusion
  92.7 2.3 %multiply_reduce_fusion.1 = (f32[1024]{0:T(1024)S(1)}, f32[1024]{0:T(1024)S(1)}, bf16[512,1024]{1,0:T(8,128)(2,1)S(1)}) fusion(f32[512]{0:T(512)S(1)} %multiply_reduce_fusion, f32[1024,512]{0,1:T(8,128)S(1)} %copy-done.110, f32[160,512]{1,0:T(8,128)S(1)} %copy-done.12, f32[160,1024]{1,0:T(8,128)S(1)} %copy-done.6, s32[1024]{0:T(1024)S(1)} %copy-done.103, ...), kind=kOutput, calls=%fused_computation.78 | convolution fusion | flops 511637504 | bytes 4151456 | tf_op jit(solution)/shard_map/dot_general | solution.py:428
  95.1 5.5 %fusion.8 = bf16[2048,1024]{1,0:T(8,128)(2,1)} fusion(bf16[2048,1024]{1,0:T(8,128)(2,1)S(1)} %copy-done.3, bf16[512,2048]{1,0:T(8,128)(2,1)S(1)} %copy-done.10, f32[1024]{0:T(1024)S(1)} %get-tuple-element.185, f32[1024]{0:T(1024)S(1)} %get-tuple-element.186, f32[2048]{0:T(1024)S(1)} %copy-done.24, f32[1024]{0:T(1024)S(1)} %copy-done.106, ...), kind=kOutput, calls=%fused_computation.11 | convolution fusion | flops 2166358016 | bytes 11558912 | tf_op jit(solution)/shard_map/dot_general | solution.py:428
  101.9 1.4 convolution_convert_fusion
  103.2 1.4 copy.33
  104.7 5.1 %fusion.10.g_ref = bf16[2048,1280]{1,0:T(8,128)(2,1)} fusion(bf16[2048,160]{1,0:T(8,128)(2,1)S(1)} %bitcast.245, bf16[2048,1024]{1,0:T(8,128)(2,1)} %fusion.8), kind=kLoop, calls=%fused_computation.13 | loop fusion | flops 15728640 | bytes 10092544 | tf_op jit(solution)/shard_map/concatenate | solution.py:495
  109.8 41.7 %shard_map.137 = f32[128,1280]{1,0:T(8,128)} custom-call(bf16[2048,1280]{1,0:T(8,128)(2,1)} %fusion.10.g_ref), custom_call_target="tpu_custom_call" | custom-call | tf_op jit(solution)/shard_map/pallas_call | solution.py:403
  151.6 1.5 slice_add_fusion
  153.9 1.2 multiply_reduce_fusion.26
  155.3 1.4 multiply_reduce_fusion.50
  156.7 1.4 multiply_reduce_fusion.49
  159.8 2.0 %broadcast_multiply_fusion.1 = (f32[128,32,32]{0,2,1:T(8,128)S(1)}, f32[128,32,32]{0,2,1:T(8,128)S(1)}, f32[128,32,32]{0,2,1:T(8,128)S(1)}, f32[128,32,32]{0,2,1...) fusion(f32[128,32,32]{0,2,1:T(8,128)S(1)} %bitcast.238, ...), kind=kLoop, calls=%fused_computation.162 | loop fusion | flops 2359296 | bytes 9970688 | tf_op jit(solution)/shard_map/transpose(jvp())/mul | solution.py:26
  162.0 1.2 broadcast_multiply_fusion
  163.4 2.3 %broadcast_multiply_fusion.2 = (f32[128,32,32]{0,2,1:T(8,128)S(1)}, f32[128,32,32]{0,2,1:T(8,128)S(1)}, f32[128,32,32]{0,2,1:T(8,128)S(1)}, f32[128,32,32]{0,2,1...) fusion(f32[128,32,32]{0,2,1:T(8,128)S(1)} %bitcast.240, ...), kind=kLoop, calls=%fused_computation.163 | loop fusion | flops 1703936 | bytes 7346688 | tf_op jit(solution)/shard_map/transpose(jvp())/mul | solution.py:26
  165.7 6.4 %pad_add_fusion = f32[128,38,38]{0,2,1:T(8,128)S(1)} fusion(f32[128,32,32]{0,2,1:T(8,128)S(1)} %get-tuple-element.91, f32[128,32,32]{0,2,1:T(8,128)S(1)} %get-tuple-element.92, f32[128,32,32]{0,2,1:T(8,128)S(1)} %get-tuple-element.93, f32[128,32,32]{0,2,1:T(8,128)S(1)} %get-tuple-element.94, f32[128,32,32]{0,2,1:T(8,128)S(1)} %get-tuple-element.95, ...), kind=kLoop, calls=%fused_computation.89 | loop fusion | flops 7762944 | bytes 23283712 | tf_op jit(solution)/shard_map/transpose(jvp())/add_any | solution.py:27
  173.2 1.4 convolution_add_fusion.1
  175.8 7.1 %fusion.27 = f32[512,2048]{1,0:T(8,128)} fusion(bf16[2048,1024]{1,0:T(8,128)(2,1)} %shard_map.135, f32[1024]{0:T(1024)S(1)} %copy-done.107, f32[1024]{0:T(1024)S(1)} %copy-done.22, f32[2048]{0:T(1024)S(1)} %copy-done.25, bf16[512,1024]{1,0:T(8,128)(2,1)} %copy-done.111), kind=kOutput, calls=%fused_computation.90 | convolution fusion | flops 2157969408 | bytes 9453568 | tf_op jit(solution)/shard_map/dot_general | solution.py:428
  183.0 3.1 %fusion.23 = f32[512,2048]{1,0:T(8,128)} fusion(bf16[512,160]{0,1:T(8,128)(2,1)S(1)} %copy-done.16, f32[2048]{0:T(1024)S(1)} %copy-done.17, bf16[2048,150]{1,0:T(8,128)(2,1)S(1)} %copy.29), kind=kOutput, calls=%fused_computation.86 | convolution fusion | flops 336527360 | bytes 4980736 | tf_op jit(solution)/shard_map/dot_general | solution.py:428
  (241 shorter events, 9.9 us)
Async XLA Ops:
  0.6 57.1 %copy-start = (bf16[512,2048]{1,0:T(8,128)(2,1)S(1)}, bf16[512,2048]{1,0:T(8,128)(2,1)}, u32[]{:S(2)}) copy-start(bf16[512,2048]{1,0:T(8,128)(2,1)} %param.13) | copy-start | bytes 6291460
  1.7 48.7 %copy-start.26 = (f32[128]{0:T(128)}, f32[128]{0:T(128)S(1)}, u32[]{:S(2)}) copy-start(f32[128]{0:T(128)S(1)} %get-tuple-element.134) | copy-start | bytes 1540
  1.7 48.7 %copy-start.28 = (f32[128]{0:T(128)}, f32[128]{0:T(128)S(1)}, u32[]{:S(2)}) copy-start(f32[128]{0:T(128)S(1)} %get-tuple-element.135) | copy-start | bytes 1540
  1.7 48.7 %copy-start.30 = (f32[128]{0:T(128)}, f32[128]{0:T(128)S(1)}, u32[]{:S(2)}) copy-start(f32[128]{0:T(128)S(1)} %get-tuple-element.136) | copy-start | bytes 1540
  1.7 48.7 %copy-start.32 = (f32[128]{0:T(128)}, f32[128]{0:T(128)S(1)}, u32[]{:S(2)}) copy-start(f32[128]{0:T(128)S(1)} %get-tuple-element.137) | copy-start | bytes 1540
  1.7 48.7 %copy-start.34 = (f32[128]{0:T(128)}, f32[128]{0:T(128)S(1)}, u32[]{:S(2)}) copy-start(f32[128]{0:T(128)S(1)} %get-tuple-element.138) | copy-start | bytes 1540
  1.7 48.7 %copy-start.36 = (f32[128]{0:T(128)}, f32[128]{0:T(128)S(1)}, u32[]{:S(2)}) copy-start(f32[128]{0:T(128)S(1)} %get-tuple-element.139) | copy-start | bytes 1540
  1.7 48.7 %copy-start.38 = (f32[128]{0:T(128)}, f32[128]{0:T(128)S(1)}, u32[]{:S(2)}) copy-start(f32[128]{0:T(128)S(1)} %get-tuple-element.140) | copy-start | bytes 1540
  1.7 48.7 %copy-start.40 = (f32[128]{0:T(128)}, f32[128]{0:T(128)S(1)}, u32[]{:S(2)}) copy-start(f32[128]{0:T(128)S(1)} %get-tuple-element.141) | copy-start | bytes 1540
  1.7 48.7 %copy-start.42 = (f32[128]{0:T(128)}, f32[128]{0:T(128)S(1)}, u32[]{:S(2)}) copy-start(f32[128]{0:T(128)S(1)} %get-tuple-element.142) | copy-start | bytes 1540
  1.8 48.7 %copy-start.44 = (f32[128]{0:T(128)}, f32[128]{0:T(128)S(1)}, u32[]{:S(2)}) copy-start(f32[128]{0:T(128)S(1)} %get-tuple-element.143) | copy-start | bytes 1540
  1.8 48.7 %copy-start.46 = (f32[128]{0:T(128)}, f32[128]{0:T(128)S(1)}, u32[]{:S(2)}) copy-start(f32[128]{0:T(128)S(1)} %get-tuple-element.144) | copy-start | bytes 1540
  1.8 48.7 %copy-start.48 = (f32[128]{0:T(128)}, f32[128]{0:T(128)S(1)}, u32[]{:S(2)}) copy-start(f32[128]{0:T(128)S(1)} %get-tuple-element.145) | copy-start | bytes 1540
  1.8 48.7 %copy-start.50 = (f32[128]{0:T(128)}, f32[128]{0:T(128)S(1)}, u32[]{:S(2)}) copy-start(f32[128]{0:T(128)S(1)} %get-tuple-element.146) | copy-start | bytes 1540
  1.8 48.7 %copy-start.52 = (f32[128]{0:T(128)}, f32[128]{0:T(128)S(1)}, u32[]{:S(2)}) copy-start(f32[128]{0:T(128)S(1)} %get-tuple-element.133) | copy-start | bytes 1540
  1.8 48.7 %copy-start.88 = (f32[128]{0:T(128)}, f32[128]{0:T(128)S(1)}, u32[]{:S(2)}) copy-start(f32[128]{0:T(128)S(1)} %get-tuple-element.147) | copy-start | bytes 1540
  1.8 48.7 %copy-start.90 = (f32[128]{0:T(128)}, f32[128]{0:T(128)S(1)}, u32[]{:S(2)}) copy-start(f32[128]{0:T(128)S(1)} %get-tuple-element.148) | copy-start | bytes 1540
  1.8 48.7 %copy-start.92 = (f32[128]{0:T(128)}, f32[128]{0:T(128)S(1)}, u32[]{:S(2)}) copy-start(f32[128]{0:T(128)S(1)} %get-tuple-element.149) | copy-start | bytes 1540
  1.8 48.7 %copy-start.94 = (f32[128]{0:T(128)}, f32[128]{0:T(128)S(1)}, u32[]{:S(2)}) copy-start(f32[128]{0:T(128)S(1)} %get-tuple-element.150) | copy-start | bytes 1540
  1.8 48.7 %copy-start.96 = (f32[128]{0:T(128)}, f32[128]{0:T(128)S(1)}, u32[]{:S(2)}) copy-start(f32[128]{0:T(128)S(1)} %get-tuple-element.151) | copy-start | bytes 1540
  3.4 47.1 %copy-start.54 = (f32[128]{0:T(128)}, f32[128]{0:T(128)S(1)}, u32[]{:S(2)}) copy-start(f32[128]{0:T(128)S(1)} %get-tuple-element.152) | copy-start | bytes 1540
  3.5 47.1 %copy-start.56 = (f32[128]{0:T(128)}, f32[128]{0:T(128)S(1)}, u32[]{:S(2)}) copy-start(f32[128]{0:T(128)S(1)} %get-tuple-element.165) | copy-start | bytes 1540
  3.5 47.1 %copy-start.58 = (f32[128]{0:T(128)}, f32[128]{0:T(128)S(1)}, u32[]{:S(2)}) copy-start(f32[128]{0:T(128)S(1)} %get-tuple-element.166) | copy-start | bytes 1540
  3.5 47.1 %copy-start.60 = (f32[128]{0:T(128)}, f32[128]{0:T(128)S(1)}, u32[]{:S(2)}) copy-start(f32[128]{0:T(128)S(1)} %get-tuple-element.167) | copy-start | bytes 1540
  3.5 47.1 %copy-start.62 = (f32[128]{0:T(128)}, f32[128]{0:T(128)S(1)}, u32[]{:S(2)}) copy-start(f32[128]{0:T(128)S(1)} %get-tuple-element.168) | copy-start | bytes 1540
  3.5 47.1 %copy-start.64 = (f32[128]{0:T(128)}, f32[128]{0:T(128)S(1)}, u32[]{:S(2)}) copy-start(f32[128]{0:T(128)S(1)} %get-tuple-element.169) | copy-start | bytes 1540
  3.5 47.1 %copy-start.66 = (f32[128]{0:T(128)}, f32[128]{0:T(128)S(1)}, u32[]{:S(2)}) copy-start(f32[128]{0:T(128)S(1)} %get-tuple-element.170) | copy-start | bytes 1540
  3.5 47.1 %copy-start.98 = (f32[128]{0:T(128)}, f32[128]{0:T(128)S(1)}, u32[]{:S(2)}) copy-start(f32[128]{0:T(128)S(1)} %get-tuple-element.153) | copy-start | bytes 1540
  3.5 47.1 %copy-start.100 = (f32[128]{0:T(128)}, f32[128]{0:T(128)S(1)}, u32[]{:S(2)}) copy-start(f32[128]{0:T(128)S(1)} %get-tuple-element.154) | copy-start | bytes 1540
  5.0 45.7 %copy-start.74 = (f32[128]{0:T(128)}, f32[128]{0:T(128)S(1)}, u32[]{:S(2)}) copy-start(f32[128]{0:T(128)S(1)} %get-tuple-element.174) | copy-start | bytes 1540
  5.0 45.7 %copy-start.76 = (f32[128]{0:T(128)}, f32[128]{0:T(128)S(1)}, u32[]{:S(2)}) copy-start(f32[128]{0:T(128)S(1)} %get-tuple-element.175) | copy-start | bytes 1540
  5.0 45.7 %copy-start.78 = (f32[128]{0:T(128)}, f32[128]{0:T(128)S(1)}, u32[]{:S(2)}) copy-start(f32[128]{0:T(128)S(1)} %get-tuple-element.176) | copy-start | bytes 1540
  (80 other events, 792.2 us)

commit v2 on v1

--- a/solution.py
+++ b/solution.py
@@ -14,19 +14,66 @@
 VMEM_LIMIT = 56 * 1024 * 1024
 
 
-def conv_apply(in_grid, kernel):
+def slide(values, rows, cols):
+    area = values.shape[1]
+    token = lax.broadcasted_iota(jnp.int32, values.shape, 1)
+    step = rows * WIN_W + cols
+    if step == 0:
+        return values
+    if cols:
+        spot = lax.rem(token, WIN_W) + cols
+        inside = (spot >= 0) & (spot < WIN_W)
+    else:
+        spot = token + step
+        inside = (spot >= 0) & (spot < area)
+    return jnp.where(inside, pltpu.roll(values, (-step) % area, 1), 0.0)
+
+
+def conv_rows(values, taps):
     half = KS // 2
-    padded = jnp.pad(in_grid, ((0, 0), (half, half), (half, half)))
-    running = jnp.zeros(in_grid.shape, in_grid.dtype)
-    for row_shift in range(KS):
-        for col_shift in range(KS):
-            tap = kernel[:, row_shift * KS + col_shift]
-            running = (
-                running
-                + tap[:, None, None]
-                * padded[:, row_shift : row_shift + WIN_H, col_shift : col_shift + WIN_W]
-            )
+    shifted = [slide(values, 0, j - half) for j in range(KS)]
+    running = None
+    for i in range(KS):
+        line = sum(taps[:, i * KS + j : i * KS + j + 1] * shifted[j] for j in range(KS))
+        line = slide(line, i - half, 0)
+        running = line if running is None else running + line
     return running
+
+
+def conv_back_kernel(grad_ref, x_ref, taps_ref, add_ref, dx_ref, dtaps_ref):
+    half = KS // 2
+    wide = dtaps_ref.shape[1]
+
+    @pl.loop(0, x_ref.shape[0] // 8)
+    def _(g):
+        own = pl.ds(pl.multiple_of(g * 8, 8), 8)
+        grad, values, taps = grad_ref[own, :], x_ref[own, :], taps_ref[own, :]
+        lifted = [slide(grad, half - i, 0) for i in range(KS)]
+        column = lax.broadcasted_iota(jnp.int32, (8, wide), 1)
+        dtaps = jnp.zeros((8, wide), jnp.float32)
+        dx = add_ref[own, :]
+        for j in range(KS):
+            line = sum(taps[:, i * KS + j : i * KS + j + 1] * lifted[i] for i in range(KS))
+            dx = dx + slide(line, 0, half - j)
+            shifted = slide(values, 0, j - half)
+            for i in range(KS):
+                whole = jnp.sum(lifted[i] * shifted, axis=1, keepdims=True)
+                dtaps = jnp.where(column == i * KS + j, whole, dtaps)
+        dx_ref[own, :] = dx
+        dtaps_ref[own, :] = dtaps
+
+
+def conv_back(grad, values, taps, add):
+    return pl.pallas_call(
+        conv_back_kernel,
+        out_shape=(
+            jax.ShapeDtypeStruct(grad.shape, jnp.float32),
+            jax.ShapeDtypeStruct(taps.shape, jnp.float32),
+        ),
+        in_specs=[pl.BlockSpec(memory_space=pltpu.VMEM)] * 4,
+        out_specs=(pl.BlockSpec(memory_space=pltpu.VMEM),) * 2,
+        compiler_params=pltpu.CompilerParams(vmem_limit_bytes=32 * 1024 * 1024),
+    )(grad, values, taps, add)
 
 
 def gelu_parts(values):
@@ -44,7 +91,7 @@
     return (z * 2 + y) * 2 + c
 
 
-def greet(devices, z, a):
+def greet(devices, z, a, between=None):
     barrier = pltpu.get_barrier_semaphore()
     for device in devices:
         pl.semaphore_signal(barrier, inc=1, device_id={"ch": device})
@@ -58,17 +105,32 @@
     def _():
         pl.semaphore_signal(barrier, inc=1, device_id={"ch": me + 4})
 
+    if between is not None:
+        between()
     count = len(devices) + jnp.where(z > 0, 1, 0) + jnp.where(z < a - 1, 1, 0)
     pl.semaphore_wait(barrier, count)
 
 
-def gather_kernel(n, x_ref, out_ref, send_sem, recv_sem):
+def gather_kernel(
+    n, x_ref, taps_ref, w_ref, head_ref, out_ref, mixed_ref, wide, conv, send_sem, recv_sem
+):
     a = n // 4
     rows = x_ref.shape[0]
     z, y, c = place(n)
     me = index_of(z, y, c)
     twin, across = index_of(z, y, 1 - c), index_of(z, 1 - y, c)
-    greet([twin, across], z, a)
+
+    def convolve():
+        wide[...] = x_ref[...].astype(jnp.float32)
+
+        @pl.loop(0, rows // 8)
+        def _(g):
+            own = pl.ds(pl.multiple_of(g * 8, 8), 8)
+            conv[own, :] = conv_rows(wide[own, :], taps_ref[own, :])
+
+        out_ref[pl.ds(pl.multiple_of(me * rows, rows), rows)] = conv[...].astype(jnp.bfloat16)
+
+    greet([twin, across], z, a, convolve)
 
     def block(b):
         return out_ref.at[pl.ds(pl.multiple_of(b * rows, rows), rows)]
@@ -82,8 +144,6 @@
             device_id={"ch": device},
         )
 
-    out_ref[pl.ds(pl.multiple_of(me * rows, rows), rows)] = x_ref[...]
-
     @pl.when(z < a - 1)
     def _():
         copy(0, me, me + 4).start()
@@ -94,6 +154,20 @@
 
     copy(2, me, across).start()
     copy(3, me, twin).start()
+
+    head = head_ref[...]
+    high = head.astype(jnp.bfloat16)
+    low = (head - high.astype(jnp.float32)).astype(jnp.bfloat16)
+    units = w_ref.shape[0]
+    part = min(units, 128)
+
+    @pl.loop(0, units // part)
+    def _(g):
+        own = pl.ds(pl.multiple_of(g * part, part), part)
+        weights = w_ref[own, :]
+        mixed_ref[own, :] = jnp.dot(
+            weights, high, preferred_element_type=jnp.float32
+        ) + jnp.dot(weights, low, preferred_element_type=jnp.float32)
 
     def from_line(s):
         below, above = me - 4 * s, me + 4 * s
@@ -157,18 +231,26 @@
             copy(1, index_of(zz, y, c), me - 4).wait_send()
 
 
-def gather(n, x):
+def gather(n, x, taps, weights, head):
     rows, cols = x.shape
     return pl.pallas_call(
         functools.partial(gather_kernel, n),
-        out_shape=jax.ShapeDtypeStruct((n * rows, cols), x.dtype),
-        in_specs=[pl.BlockSpec(memory_space=pltpu.VMEM)],
-        out_specs=pl.BlockSpec(memory_space=pltpu.VMEM),
-        scratch_shapes=[pltpu.SemaphoreType.DMA((4, n)), pltpu.SemaphoreType.DMA((n,))],
+        out_shape=(
+            jax.ShapeDtypeStruct((n * rows, cols), x.dtype),
+            jax.ShapeDtypeStruct((weights.shape[0], head.shape[1]), jnp.float32),
+        ),
+        in_specs=[pl.BlockSpec(memory_space=pltpu.VMEM)] * 4,
+        out_specs=(pl.BlockSpec(memory_space=pltpu.VMEM),) * 2,
+        scratch_shapes=[
+            pltpu.VMEM((rows, cols), jnp.float32),
+            pltpu.VMEM((rows, cols), jnp.float32),
+            pltpu.SemaphoreType.DMA((4, n)),
+            pltpu.SemaphoreType.DMA((n,)),
+        ],
         compiler_params=pltpu.CompilerParams(
             collective_id=0, has_side_effects=True, vmem_limit_bytes=VMEM_LIMIT
         ),
-    )(x)
+    )(x, taps, weights, head)
 
 
 def total_kernel(n, x_ref, out_ref, buf, from_twin, acc, slots, sums, t_sem, r_sem, g_sem, f_sem):
@@ -285,7 +367,8 @@
 
 
 def scatter_kernel(
-    n, g_ref, out_ref, t_in, y_in, u_in, d_in, y_out, z_out, t_sem, y_sem, u_sem, d_sem, zs_sem
+    n, conv_ref, w_ref, p_ref, rows_ref, seen_ref, out_ref,
+    g_ref, t_in, y_in, u_in, d_in, y_out, z_out, t_sem, y_sem, u_sem, d_sem, zs_sem
 ):
     a = n // 4
     rows = out_ref.shape[0]
@@ -331,11 +414,19 @@
             device_id={"ch": device},
         )
 
-    for k in range(a):
-        to_twin(order(k), 1 - y, 1 - c).start()
-    for k in range(a):
-        to_twin(order(k), y, 1 - c).start()
-    for k in range(a):
+    tokens = conv_ref.shape[1]
+    tok_mean, inv_std = rows_ref[0:1, :], rows_ref[1:2, :]
+    mean_gained, mean_both = rows_ref[2:3, :], rows_ref[3:4, :]
+
+    def fill(zz, side, core):
+        mine = own(index_of(zz, side, core))
+        grad = jnp.dot(w_ref[mine, :], p_ref[...], preferred_element_type=jnp.float32)
+        normed = (conv_ref[mine, :].astype(jnp.float32) - tok_mean) * inv_std
+        term = (grad - mean_gained - normed * mean_both) * inv_std
+        g_ref[mine, :tokens] = term.astype(jnp.bfloat16)
+        g_ref[mine, tokens:] = seen_ref[mine, :]
+
+    def cross(k):
         zz = order(k)
         to_twin(zz, 1 - y, c).wait_recv()
         y_out[k] = (
@@ -343,8 +434,23 @@
             + t_in[zz * 2 + 1 - y].astype(jnp.float32)
         ).astype(jnp.bfloat16)
         to_across(k, zz).start()
+
+    for k in range(a):
+        fill(order(k), 1 - y, 1 - c)
+        to_twin(order(k), 1 - y, 1 - c).start()
+        fill(order(k), 1 - y, c)
+        if k > 0:
+            cross(k - 1)
+    fill(order(0), y, 1 - c)
+    to_twin(order(0), y, 1 - c).start()
+    cross(a - 1)
+    fill(order(0), y, c)
     for k in range(a):
         zz = order(k)
+        if k < a - 1:
+            fill(order(k + 1), y, 1 - c)
+            to_twin(order(k + 1), y, 1 - c).start()
+            fill(order(k + 1), y, c)
         to_twin(zz, y, c).wait_recv()
         to_across(k, zz).wait_recv()
         term = (
@@ -397,15 +503,16 @@
             along(k, zz, u_in, u_sem, me).wait_send()
 
 
-def scatter(n, g):
-    rows, cols = g.shape[0] // n, g.shape[1]
+def scatter(n, conv_all, weights, pre_grad, token_rows, seen):
+    rows, cols = conv_all.shape[0] // n, conv_all.shape[1] + seen.shape[1]
     a = n // 4
     return pl.pallas_call(
         functools.partial(scatter_kernel, n),
         out_shape=jax.ShapeDtypeStruct((rows, cols), jnp.float32),
-        in_specs=[pl.BlockSpec(memory_space=pltpu.VMEM)],
+        in_specs=[pl.BlockSpec(memory_space=pltpu.VMEM)] * 5,
         out_specs=pl.BlockSpec(memory_space=pltpu.VMEM),
         scratch_shapes=[
+            pltpu.VMEM((n * rows, cols), jnp.bfloat16),
             pltpu.VMEM((n // 2, rows, cols), jnp.bfloat16),
             pltpu.VMEM((a, rows, cols), jnp.bfloat16),
             pltpu.VMEM((a, rows, cols), jnp.bfloat16),
@@ -421,7 +528,7 @@
         compiler_params=pltpu.CompilerParams(
             collective_id=2, has_side_effects=True, vmem_limit_bytes=VMEM_LIMIT
         ),
-    )(g)
+    )(conv_all, weights, pre_grad, token_rows, seen)
 
 
 def dot(lhs, rhs, over, precision=None):
@@ -437,9 +544,10 @@
     channels, class_count = w_head.shape
     row_offset = lax.axis_index("ch") * my_rows
     inputs_wide = features.astype(jnp.float32)
-    in_grid = inputs_wide.reshape(my_rows, WIN_H, WIN_W)
-    conv_out = conv_apply(in_grid, dw_weight).reshape(my_rows, tok_count).astype(jnp.bfloat16)
-    conv_all = gather(n, conv_out)
+    classes = -(-class_count // max(n, 16)) * max(n, 16)
+    head_pad = jnp.pad(w_head, ((0, 0), (0, classes - class_count)))
+    scaled_head = layer_scale[:, None] * head_pad.astype(jnp.float32)
+    conv_all, mixed = gather(n, features, dw_weight, w_out, scaled_head)
     conv_wide = conv_all.astype(jnp.float32)
     tok_mean = jnp.mean(conv_wide, axis=0)
     centered = conv_wide - tok_mean[None, :]
@@ -450,14 +558,9 @@
     gelu_out, gelu_slope = gelu_parts(pre_act)
     hidden = gelu_out.astype(jnp.bfloat16)
 
-    classes = -(-class_count // max(n, 16)) * max(n, 16)
-    head_pad = jnp.pad(w_head, ((0, 0), (0, classes - class_count)))
-    head_wide = head_pad.astype(jnp.float32)
     my_scale = lax.dynamic_slice_in_dim(layer_scale, row_offset, my_rows, 0)
     my_head = lax.dynamic_slice_in_dim(head_pad, row_offset, my_rows, 0)
     my_head_wide = my_head.astype(jnp.float32)
-    scaled_head = layer_scale[:, None] * head_wide
-    mixed = dot(w_out.astype(jnp.float32), scaled_head, (1, 0), fine)
     part = dot(mixed, hidden.astype(jnp.float32), (0, 0), fine) + dot(my_head, features, (0, 0))
     logits = total(n, part)
 
@@ -485,28 +588,17 @@
     gain_rows = jnp.sum(w_in.astype(jnp.float32) * norm_gain[None, :], axis=1)
     mean_gained = jnp.sum(gain_rows[:, None] * pre_grad_wide, axis=0) / channels
     mean_both = jnp.sum(pre_act * pre_grad_wide, axis=0) / channels
-    norm_grad = dot(w_in, pre_grad, (0, 0))
-    conv_term = (
-        norm_gain[:, None] * norm_grad
-        - mean_gained[None, :]
-        - (centered * inv_std[None, :]) * mean_both[None, :]
-    ) * inv_std[None, :]
+    weights = (w_in.astype(jnp.float32) * norm_gain[None, :]).astype(jnp.bfloat16).T
     width = -(-classes // 128) * 128
-    payload = jnp.concatenate(
-        [
-            conv_term.astype(jnp.bfloat16),
-            jnp.pad(branch_seen, ((0, 0), (0, width - classes))),
-        ],
-        axis=1,
-    )
-    landed = scatter(n, payload)
+    token_rows = jnp.stack([tok_mean, inv_std, mean_gained, mean_both])
+    token_rows = jnp.pad(token_rows, ((0, 4), (0, 0)))
+    branch_seen = jnp.pad(branch_seen, ((0, 0), (0, width - classes)))
+    landed = scatter(n, conv_all, weights, pre_grad, token_rows, branch_seen)
     conv_grad = landed[:, :tok_count]
     my_seen = landed[:, tok_count : tok_count + class_count]
     d_head = dot(inputs_wide, logit_grad, (1, 1), fine)[:, :class_count] + my_scale[:, None] * my_seen
     d_scale = jnp.sum(my_head_wide[:, :class_count] * my_seen, axis=1)
-    unused, pullback = jax.vjp(conv_apply, in_grid, dw_weight)
-    grid_grad, d_dw = pullback(conv_grad.reshape(my_rows, WIN_H, WIN_W))
-    d_features = out_grad + grid_grad.reshape(my_rows, tok_count)
+    d_features, d_dw = conv_back(conv_grad, inputs_wide, dw_weight, out_grad)
     return (d_features, d_dw, d_scale, d_w_in, d_w_out, d_head, mean_loss)
 
 

time: 188 us -> 174 us (0.926)
  Pallas kernels: 100 us -> 126 us
  other arithmetic: 37.1 us -> 12.4 us
  matrix products: 33.4 us -> 19.7 us
    pallas_call x1 -> x2, Pallas kernels: 35.5 us -> 60.6 us  [the longest x1 44 us: gather(): pl.pallas_call(functools.partial(gather_kernel, n), out_shape=(jax.ShapeD...]
    dot_general x11 -> x9, matrix products: 29.3 us -> 15.9 us  [dot(): lax.dot_general(lhs, rhs, ((over[:1], over[1:]), ((), ())), precision=pre...]
    add_any x3 -> x0, other arithmetic: 7.57 us -> none  [the longest x2 6.8 us: conv_apply(): padded[:, row_shift:row_shift + WIN_H, col_shift:col_shift + WIN_W]]
    unnamed x226 -> x53, local copies, waits for them, and re-layouts: 4.56 us -> 9.78 us
    concatenate x1 -> x0, other arithmetic: 5.11 us -> none  [per_device(): jnp.concatenate([conv_term.astype(jnp.bfloat16), jnp.pad(branch_seen, ((0...]
    convert_element_type x1, other arithmetic: 4.81 us -> 0.04 us  [per_device(): inputs_wide = features.astype(jnp.float32)]
    reduce_sum x4 -> x0, other arithmetic: 4.63 us -> none  [conv_apply(): tap[:, None, None]]
    mul x3 -> x0, local copies, waits for them, and re-layouts: 4.03 us -> none  [conv_apply(): tap[:, None, None]]
where the time goes in v2:
time: 174 us
  Pallas kernels  126 us (72%)
  matrix products  19.7 us (11%)
  local copies, waits for them, and re-layouts  12.6 us (7%)
  other arithmetic  12.4 us (7%)
  between operations  2.7 us (2%)
    pallas_call x1, Pallas kernels, scatter(): pl.pallas_call(functools.partial(scatter_kernel, n), out_shape=jax.ShapeD...  44.3 us
    pallas_call x1, Pallas kernels, gather(): pl.pallas_call(functools.partial(gather_kernel, n), out_shape=(jax.ShapeD...  44 us
    pallas_call x1, Pallas kernels, total(): pl.pallas_call(functools.partial(total_kernel, n), out_shape=jax.ShapeDty...  21.5 us
    pallas_call x1, Pallas kernels, conv_back(): pl.pallas_call(conv_back_kernel, out_shape=(jax.ShapeDtypeStruct(grad.sha...  16.6 us
    dot_general x9, matrix products, dot(): lax.dot_general(lhs, rhs, ((over[:1], over[1:]), ((), ())), precision=pre...  15.9 us
    unnamed x53, local copies, waits for them, and re-layouts  9.78 us
    dot_general x1, matrix products, per_device(): pre_act = jnp.dot(w_in, norm_out, preferred_element_type=jnp.float32)  3.81 us

profile of v2, /device:TPU:0, one launch (start us, length us, event | category | flops | bytes accessed | tf_op | source)
XLA Modules:
  0.0 173.7 jit_solution(13059341971092916265)
XLA Ops:
  0.6 1.5 copy.24.taps_ref
  2.1 1.4 copy.23
  3.5 2.4 %convert_multiply_fusion.1.head_ref = f32[2048,160]{1,0:T(8,128)} fusion(f32[2048]{0:T(1024)} %param.11, bf16[2048,150]{1,0:T(8,128)(2,1)S(1)} %copy.23), kind=kLoop, calls=%fused_computation.27 | loop fusion | flops 655360 | bytes 1933312 | tf_op jit(solution)/shard_map/mul | solution.py:549
  5.9 44.0 %shard_map.135 = (bf16[2048,1024]{1,0:T(8,128)(2,1)}, f32[512,160]{1,0:T(8,128)}) custom-call(bf16[128,1024]{1,0:T(8,128)(2,1)} %x_ref.1, f32[128,49]{1,0:T(8,128)} %copy.24.taps_ref, bf16[512,2048]{1,0:T(8,128)(2,1)} %w_ref.1, f32[2048,160]{1,0:T(8,128)} %convert_multiply_fusion.1.head_ref), custom_call_target="tpu_custom_call" | custom-call | tf_op jit(solution)/shard_map/pallas_call | solution.py:236
  49.9 2.9 %copy.25 = bf16[512,2048]{0,1:T(8,128)(2,1)S(1)} copy(bf16[512,2048]{1,0:T(8,128)(2,1)} %param.12) | data formatting | bytes 4194304 | tf_op args[4]
  52.8 2.4 %fusion.5 = (f32[512]{0:T(512)}, bf16[2048,512]{1,0:T(8,128)(2,1)}) fusion(bf16[512,2048]{0,1:T(8,128)(2,1)S(1)} %copy.25, f32[2048]{0:T(1024)S(1)} %copy-done.16), kind=kLoop, calls=%fused_computation.8 | loop fusion | flops 4193792 | bytes 4204544 | tf_op jit(solution)/shard_map/reduce_sum | solution.py:588
  55.8 0.7 convert_reduce_fusion
  56.5 1.2 fusion.2
  58.0 3.8 %fusion.16 = (bf16[512,1024]{1,0:T(8,128)(2,1)S(1)}, f32[1024,512]{0,1:T(8,128)}) fusion(bf16[512,2048]{1,0:T(8,128)(2,1)S(1)} %copy-done.7, bf16[2048,1024]{1,0:T(8,128)(2,1)S(1)} %copy-done.1, f32[1024]{0:T(1024)S(1)} %add_rsqrt_fusion, f32[1024]{0:T(1024)S(1)} %broadcast_multiply_fusion.2, f32[2048]{0:T(1024)S(1)} %copy-done.16), kind=kOutput, calls=%fused_computation.24 | convolution fusion | flops 2160590848 | bytes 9453568 | tf_op jit(solution)/shard_map/dot_general | solution.py:557
  61.9 0.6 fusion.27
  62.8 1.1 convolution_add_fusion.x_ref
  63.9 21.5 %shard_map.136 = f32[160,1024]{1,0:T(8,128)} custom-call(f32[160,1024]{1,0:T(8,128)} %convolution_add_fusion.x_ref), custom_call_target="tpu_custom_call" | custom-call | tf_op jit(solution)/shard_map/pallas_call | solution.py:347
  85.5 1.2 select_reduce_fusion.1
  86.7 1.3 select_reduce_fusion
  88.1 4.4 %multiply_reduce_fusion = (f32[1024]{0:T(1024)S(1)}, f32[1024]{0:T(1024)S(1)}, bf16[512,1024]{1,0:T(8,128)(2,1)}) fusion(f32[512]{0:T(512)S(1)} %copy-done.20, f32[1024,512]{0,1:T(8,128)S(1)} %copy-done.23, f32[512,160]{1,0:T(8,128)S(1)} %copy-done.11, f32[160,1024]{1,0:T(8,128)} %shard_map.136, s32[1024]{0:T(1024)S(1)} %copy-done.18, ...), kind=kOutput, calls=%fused_computation.26 | convolution fusion | flops 511637504 | bytes 4151456 | tf_op jit(solution)/shard_map/dot_general | solution.py:535
  92.5 0.6 select_maximum_fusion.rows_ref
  93.1 0.6 convolution_convert_fusion.1
  93.7 0.7 copy-done.9
  94.8 0.5 convolution_convert_fusion
  95.3 0.5 copy.26
  95.8 1.2 pad.14.seen_ref
  97.0 44.3 %shard_map.137 = f32[128,1280]{1,0:T(8,128)} custom-call(bf16[2048,1024]{1,0:T(8,128)(2,1)} %get-tuple-element.11.conv_ref, bf16[2048,512]{1,0:T(8,128)(2,1)} %get-tuple-element.34.w_ref, bf16[512,1024]{1,0:T(8,128)(2,1)} %get-tuple-element.35.p_ref, f32[8,1024]{1,0:T(8,128)} %select_maximum_fusion.rows_ref, bf16[2048,256]{1,0:T(8,128)(2,1)} %pad.14.seen_ref), custom_call_target="tpu_custom_call" | custom-call | tf_op jit(solution)/shard_map/pallas_call | solution.py:509
  141.2 1.1 slice.15.grad_ref
  142.4 0.6 fusion.26.add_ref
  143.2 16.6 %shard_map.138 = (f32[128,1024]{1,0:T(8,128)}, f32[128,49]{1,0:T(8,128)S(1)}) custom-call(f32[128,1024]{1,0:T(8,128)S(1)} %slice.15.grad_ref, f32[128,1024]{1,0:T(8,128)S(1)} %convert_element_type.63.x_ref, f32[128,49]{1,0:T(8,128)S(1)} %copy-done, f32[128,1024]{1,0:T(8,128)S(1)} %fusion.26.add_ref), custom_call_target="tpu_custom_call" | custom-call | tf_op jit(solution)/shard_map/pallas_call | solution.py:67
  159.7 0.7 copy.29
  160.4 0.5 convolution_bitcast_fusion
  161.1 1.8 %slice_add_fusion = (f32[128,150]{1,0:T(8,128)S(1)}, f32[128]{0:T(128)}) fusion(f32[128,160]{1,0:T(8,128)S(1)} %convolution_bitcast_fusion, f32[128,1280]{1,0:T(8,128)} %shard_map.137, f32[128]{0:T(128)S(1)} %dynamic_slice.7, s32[]{:T(128)S(6)} %select_n.11, bf16[2048,150]{1,0:T(8,128)(2,1)S(1)} %copy.23), kind=kLoop, calls=%fused_computation.44 | loop fusion | flops 95872 | bytes 845828 | tf_op jit(solution)/shard_map/add | solution.py:599
  162.9 4.6 %fusion.20 = f32[512,2048]{1,0:T(8,128)} fusion(bf16[512,1024]{1,0:T(8,128)(2,1)S(1)} %copy-done.8, bf16[2048,1024]{1,0:T(8,128)(2,1)S(1)} %copy-done.2, f32[1024]{0:T(1024)S(1)} %copy-done.15, f32[1024]{0:T(1024)S(1)} %broadcast_multiply_fusion.2, f32[2048]{0:T(1024)S(1)} %copy-done.17), kind=kOutput, calls=%fused_computation.35 | convolution fusion | flops 2157969408 | bytes 9453568 | tf_op jit(solution)/shard_map/dot_general | solution.py:535
  167.5 3.1 %fusion.18 = f32[512,2048]{1,0:T(8,128)} fusion(bf16[512,160]{0,1:T(8,128)(2,1)S(1)} %copy-done.10, f32[2048]{0:T(1024)S(1)} %copy-done.12, bf16[2048,150]{1,0:T(8,128)(2,1)S(1)} %copy.23), kind=kOutput, calls=%fused_computation.31 | convolution fusion | flops 336527360 | bytes 4980736 | tf_op jit(solution)/shard_map/dot_general | solution.py:535
  170.6 0.7 copy.30
  171.4 0.6 subtract_reduce_fusion
  (53 shorter events, 2.1 us)
Async XLA Ops:
  49.9 2.9 %copy-start.16 = (f32[2048]{0:T(1024)S(1)}, f32[2048]{0:T(1024)}, u32[]{:S(2)}) copy-start(f32[2048]{0:T(1024)} %param.10) | copy-start | bytes 24580
  52.8 2.9 %copy-start.1 = (bf16[2048,1024]{1,0:T(8,128)(2,1)S(1)}, bf16[2048,1024]{1,0:T(8,128)(2,1)}, u32[]{:S(2)}) copy-start(bf16[2048,1024]{1,0:T(8,128)(2,1)} %get-tuple-element.11.conv_ref) | copy-start | bytes 12582916
  56.4 1.6 copy-start.7
  58.0 3.8 %copy-start.13 = (f32[1024]{0:T(1024)}, f32[1024]{0:T(1024)S(1)}, u32[]{:S(2)}) copy-start(f32[1024]{0:T(1024)S(1)} %add_rsqrt_fusion) | copy-start | bytes 12292
  58.0 3.8 %copy-start.11 = (f32[512,160]{1,0:T(8,128)S(1)}, f32[512,160]{1,0:T(8,128)}, u32[]{:S(2)}) copy-start(f32[512,160]{1,0:T(8,128)} %get-tuple-element.12) | copy-start | bytes 983044
  61.8 1.0 copy-start.5
  62.8 23.9 %copy-start.18 = (s32[1024]{0:T(1024)S(1)}, s32[1024]{0:T(1024)}, u32[]{:S(2)}) copy-start(s32[1024]{0:T(1024)} %param.15) | copy-start | bytes 12292
  62.8 25.2 %copy-start.20 = (f32[512]{0:T(512)S(1)}, f32[512]{0:T(512)}, u32[]{:S(2)}) copy-start(f32[512]{0:T(512)} %get-tuple-element.33) | copy-start | bytes 6148
  62.8 25.3 %copy-start.23 = (f32[1024,512]{0,1:T(8,128)S(1)}, f32[1024,512]{0,1:T(8,128)}, u32[]{:S(2)}) copy-start(f32[1024,512]{0,1:T(8,128)} %get-tuple-element.39) | copy-start | bytes 6291460
  85.4 7.7 %copy-start.21 = (pred[160]{0:T(512)(128)(4,1)}, pred[160]{0:T(512)(128)(4,1)S(1)}, u32[]{:S(2)}) copy-start(pred[160]{0:T(512)(128)(4,1)S(1)} %iota_compare_fusion.2) | copy-start | bytes 484
  88.1 4.4 %copy-start.14 = (f32[1024]{0:T(1024)S(1)}, f32[1024]{0:T(1024)}, u32[]{:S(2)}) copy-start(f32[1024]{0:T(1024)} %copy-done.13) | copy-start | bytes 12292
  88.1 5.0 %copy-start.4 = (f32[160,1024]{1,0:T(8,128)S(1)}, f32[160,1024]{1,0:T(8,128)}, u32[]{:S(2)}) copy-start(f32[160,1024]{1,0:T(8,128)} %shard_map.136) | copy-start | bytes 1966084
  93.1 1.7 copy-start.3
  93.7 0.7 copy-start.9
  97.0 45.4 %copy-start.6 = (bf16[128,1024]{1,0:T(8,128)(2,1)S(1)}, bf16[128,1024]{1,0:T(8,128)(2,1)}, u32[]{:S(2)}) copy-start(bf16[128,1024]{1,0:T(8,128)(2,1)} %x_ref.1) | copy-start | bytes 786436
  97.0 45.4 %copy-start.19 = (s32[1024]{0:T(1024)S(1)}, s32[1024]{0:T(1024)}, u32[]{:S(2)}) copy-start(s32[1024]{0:T(1024)} %param.15) | copy-start | bytes 12292
  97.0 45.5 %copy-start.22 = (pred[160]{0:T(512)(128)(4,1)S(1)}, pred[160]{0:T(512)(128)(4,1)}, u32[]{:S(2)}) copy-start(pred[160]{0:T(512)(128)(4,1)} %copy-done.21) | copy-start | bytes 484
  142.3 0.8 copy-start
  143.2 19.8 %copy-start.8 = (bf16[512,1024]{1,0:T(8,128)(2,1)S(1)}, bf16[512,1024]{1,0:T(8,128)(2,1)}, u32[]{:S(2)}) copy-start(bf16[512,1024]{1,0:T(8,128)(2,1)} %get-tuple-element.35.p_ref) | copy-start | bytes 3145732
  159.7 1.2 copy-start.12
  160.4 2.5 %copy-start.2 = (bf16[2048,1024]{1,0:T(8,128)(2,1)S(1)}, bf16[2048,1024]{1,0:T(8,128)(2,1)}, u32[]{:S(2)}) copy-start(bf16[2048,1024]{1,0:T(8,128)(2,1)} %get-tuple-element.11.conv_ref) | copy-start | bytes 12582916
  160.4 2.5 %copy-start.15 = (f32[1024]{0:T(1024)S(1)}, f32[1024]{0:T(1024)}, u32[]{:S(2)}) copy-start(f32[1024]{0:T(1024)} %copy-done.13) | copy-start | bytes 12292
  160.4 2.5 %copy-start.17 = (f32[2048]{0:T(1024)S(1)}, f32[2048]{0:T(1024)}, u32[]{:S(2)}) copy-start(f32[2048]{0:T(1024)} %param.10) | copy-start | bytes 24580
  162.9 4.6 %copy-start.10 = (bf16[512,160]{0,1:T(8,128)(2,1)S(1)}, bf16[512,160]{0,1:T(8,128)(2,1)}, u32[]{:S(2)}) copy-start(bf16[512,160]{0,1:T(8,128)(2,1)} %copy-done.9) | copy-start | bytes 491524

commit v3 on v2

--- a/solution.py
+++ b/solution.py
@@ -20,12 +20,8 @@
     step = rows * WIN_W + cols
     if step == 0:
         return values
-    if cols:
-        spot = lax.rem(token, WIN_W) + cols
-        inside = (spot >= 0) & (spot < WIN_W)
-    else:
-        spot = token + step
-        inside = (spot >= 0) & (spot < area)
+    spot = (token & (WIN_W - 1)) if cols else token
+    inside = (spot < (WIN_W if cols else area) - step) if step > 0 else (spot >= -step)
     return jnp.where(inside, pltpu.roll(values, (-step) % area, 1), 0.0)
 
 
@@ -116,6 +112,8 @@
 ):
     a = n // 4
     rows = x_ref.shape[0]
+    parts = 2 if rows % 32 == 0 else 1
+    chunk = rows // parts
     z, y, c = place(n)
     me = index_of(z, y, c)
     twin, across = index_of(z, y, 1 - c), index_of(z, 1 - y, c)
@@ -123,37 +121,48 @@
     def convolve():
         wide[...] = x_ref[...].astype(jnp.float32)
 
-        @pl.loop(0, rows // 8)
+        convolve_part(0)
+
+    def convolve_part(h):
+        first = h * chunk
+
+        @pl.loop(0, chunk // 8)
         def _(g):
-            own = pl.ds(pl.multiple_of(g * 8, 8), 8)
+            own = pl.ds(pl.multiple_of(first + g * 8, 8), 8)
             conv[own, :] = conv_rows(wide[own, :], taps_ref[own, :])
 
-        out_ref[pl.ds(pl.multiple_of(me * rows, rows), rows)] = conv[...].astype(jnp.bfloat16)
+        out_ref[pl.ds(pl.multiple_of(me * rows + first, chunk), chunk)] = conv[
+            first : first + chunk
+        ].astype(jnp.bfloat16)
 
     greet([twin, across], z, a, convolve)
 
-    def block(b):
-        return out_ref.at[pl.ds(pl.multiple_of(b * rows, rows), rows)]
-
-    def copy(kind, b, device):
+    def copy(kind, b, device, h):
+        piece = out_ref.at[pl.ds(pl.multiple_of(b * rows + h * chunk, chunk), chunk)]
         return pltpu.make_async_remote_copy(
-            src_ref=block(b),
-            dst_ref=block(b),
-            send_sem=send_sem.at[kind, b],
-            recv_sem=recv_sem.at[b],
+            src_ref=piece,
+            dst_ref=piece,
+            send_sem=send_sem.at[kind, b * parts + h],
+            recv_sem=recv_sem.at[b * parts + h],
             device_id={"ch": device},
         )
 
-    @pl.when(z < a - 1)
-    def _():
-        copy(0, me, me + 4).start()
-
-    @pl.when(z > 0)
-    def _():
-        copy(1, me, me - 4).start()
-
-    copy(2, me, across).start()
-    copy(3, me, twin).start()
+    def send_own(h):
+        @pl.when(z < a - 1)
+        def _():
+            copy(0, me, me + 4, h).start()
+
+        @pl.when(z > 0)
+        def _():
+            copy(1, me, me - 4, h).start()
+
+        copy(2, me, across, h).start()
+        copy(3, me, twin, h).start()
+
+    for h in range(parts):
+        if h > 0:
+            convolve_part(h)
+        send_own(h)
 
     head = head_ref[...]
     high = head.astype(jnp.bfloat16)
@@ -169,35 +178,35 @@
             weights, high, preferred_element_type=jnp.float32
         ) + jnp.dot(weights, low, preferred_element_type=jnp.float32)
 
-    def from_line(s):
+    def from_line(s, h):
         below, above = me - 4 * s, me + 4 * s
 
         @pl.when(z >= s)
         def _():
-            copy(0, below, me).wait_recv()
+            copy(0, below, me, h).wait_recv()
 
             @pl.when(z < a - 1)
             def _():
-                copy(0, below, me + 4).start()
-
-            copy(2, below, across).start()
-            copy(3, below, twin).start()
+                copy(0, below, me + 4, h).start()
+
+            copy(2, below, across, h).start()
+            copy(3, below, twin, h).start()
 
         @pl.when(z + s < a)
         def _():
-            copy(1, above, me).wait_recv()
+            copy(1, above, me, h).wait_recv()
 
             @pl.when(z > 0)
             def _():
-                copy(1, above, me - 4).start()
-
-            copy(2, above, across).start()
-            copy(3, above, twin).start()
-
-    def from_across(s):
+                copy(1, above, me - 4, h).start()
+
+            copy(2, above, across, h).start()
+            copy(3, above, twin, h).start()
+
+    def from_across(s, h):
         def take(b):
-            copy(2, b, across).wait_recv()
-            copy(3, b, twin).start()
+            copy(2, b, across, h).wait_recv()
+            copy(3, b, twin, h).start()
 
         if s == 0:
             take(across)
@@ -212,23 +221,26 @@
             take(across + 4 * s)
 
     for s in range(1, a):
-        from_line(s)
-        from_across(s - 1)
-    from_across(a - 1)
-
-    for q in range(n // 2):
-        copy(3, q * 2 + 1 - c, twin).wait_recv()
-        copy(3, q * 2 + c, twin).wait_send()
-    for zz in range(a):
-        copy(2, index_of(zz, y, c), across).wait_send()
-
-        @pl.when((z < a - 1) & (zz <= z))
-        def _():
-            copy(0, index_of(zz, y, c), me + 4).wait_send()
-
-        @pl.when((z > 0) & (zz >= z))
-        def _():
-            copy(1, index_of(zz, y, c), me - 4).wait_send()
+        for h in range(parts):
+            from_line(s, h)
+            from_across(s - 1, h)
+    for h in range(parts):
+        from_across(a - 1, h)
+
+    for h in range(parts):
+        for q in range(n // 2):
+            copy(3, q * 2 + 1 - c, twin, h).wait_recv()
+            copy(3, q * 2 + c, twin, h).wait_send()
+        for zz in range(a):
+            copy(2, index_of(zz, y, c), across, h).wait_send()
+
+            @pl.when((z < a - 1) & (zz <= z))
+            def _():
+                copy(0, index_of(zz, y, c), me + 4, h).wait_send()
+
+            @pl.when((z > 0) & (zz >= z))
+            def _():
+                copy(1, index_of(zz, y, c), me - 4, h).wait_send()
 
 
 def gather(n, x, taps, weights, head):
@@ -244,8 +256,8 @@
         scratch_shapes=[
             pltpu.VMEM((rows, cols), jnp.float32),
             pltpu.VMEM((rows, cols), jnp.float32),
-            pltpu.SemaphoreType.DMA((4, n)),
-            pltpu.SemaphoreType.DMA((n,)),
+            pltpu.SemaphoreType.DMA((4, 2 * n)),
+            pltpu.SemaphoreType.DMA((2 * n,)),
         ],
         compiler_params=pltpu.CompilerParams(
             collective_id=0, has_side_effects=True, vmem_limit_bytes=VMEM_LIMIT
@@ -367,7 +379,8 @@
 
 
 def scatter_kernel(
-    n, conv_ref, w_ref, p_ref, rows_ref, seen_ref, out_ref,
+    n, conv_ref, w_ref, p_ref, rows_ref, seen_ref, norm_ref, unit_ref, head_ref,
+    out_ref, d_in_ref, d_out_ref,
     g_ref, t_in, y_in, u_in, d_in, y_out, z_out, t_sem, y_sem, u_sem, d_sem, zs_sem
 ):
     a = n // 4
@@ -415,6 +428,8 @@
         )
 
     tokens = conv_ref.shape[1]
+    slabs = min(a, 4)
+    deep = p_ref.shape[0] // slabs
     tok_mean, inv_std = rows_ref[0:1, :], rows_ref[1:2, :]
     mean_gained, mean_both = rows_ref[2:3, :], rows_ref[3:4, :]
 
@@ -451,6 +466,10 @@
             fill(order(k + 1), y, 1 - c)
             to_twin(order(k + 1), y, 1 - c).start()
             fill(order(k + 1), y, c)
+        if k < slabs:
+            slab = pl.ds(k * deep, deep)
+            d_in_ref[slab, :] = dot(p_ref[slab, :], norm_ref[...], (1, 1))
+            d_out_ref[slab, :] = dot(unit_ref[slab, :], head_ref[...], (1, 1))
         to_twin(zz, y, c).wait_recv()
         to_across(k, zz).wait_recv()
         term = (
@@ -503,14 +522,18 @@
             along(k, zz, u_in, u_sem, me).wait_send()
 
 
-def scatter(n, conv_all, weights, pre_grad, token_rows, seen):
+def scatter(n, conv_all, weights, pre_grad, token_rows, seen, norm_out, units, head):
     rows, cols = conv_all.shape[0] // n, conv_all.shape[1] + seen.shape[1]
     a = n // 4
     return pl.pallas_call(
         functools.partial(scatter_kernel, n),
-        out_shape=jax.ShapeDtypeStruct((rows, cols), jnp.float32),
-        in_specs=[pl.BlockSpec(memory_space=pltpu.VMEM)] * 5,
-        out_specs=pl.BlockSpec(memory_space=pltpu.VMEM),
+        out_shape=(
+            jax.ShapeDtypeStruct((rows, cols), jnp.float32),
+            jax.ShapeDtypeStruct((pre_grad.shape[0], norm_out.shape[0]), jnp.float32),
+            jax.ShapeDtypeStruct((units.shape[0], head.shape[0]), jnp.float32),
+        ),
+        in_specs=[pl.BlockSpec(memory_space=pltpu.VMEM)] * 8,
+        out_specs=(pl.BlockSpec(memory_space=pltpu.VMEM),) * 3,
         scratch_shapes=[
             pltpu.VMEM((n * rows, cols), jnp.bfloat16),
             pltpu.VMEM((n // 2, rows, cols), jnp.bfloat16),
@@ -528,7 +551,7 @@
         compiler_params=pltpu.CompilerParams(
             collective_id=2, has_side_effects=True, vmem_limit_bytes=VMEM_LIMIT
         ),
-    )(conv_all, weights, pre_grad, token_rows, seen)
+    )(conv_all, weights, pre_grad, token_rows, seen, norm_out, units, head)
 
 
 def dot(lhs, rhs, over, precision=None):
@@ -580,11 +603,9 @@
     seen = dot(hidden, grad_narrow, (1, 1))
     hidden_grad = dot(mixed, logit_grad, (1, 0), fine)
     seen_narrow = seen.astype(jnp.bfloat16)
-    d_w_out = dot(seen_narrow, scaled_head.astype(jnp.bfloat16), (1, 1))
     branch_seen = dot(w_out, seen_narrow, (0, 0)).astype(jnp.bfloat16)
     pre_grad_wide = hidden_grad * gelu_slope
     pre_grad = pre_grad_wide.astype(jnp.bfloat16)
-    d_w_in = dot(pre_grad, norm_out, (1, 1))
     gain_rows = jnp.sum(w_in.astype(jnp.float32) * norm_gain[None, :], axis=1)
     mean_gained = jnp.sum(gain_rows[:, None] * pre_grad_wide, axis=0) / channels
     mean_both = jnp.sum(pre_act * pre_grad_wide, axis=0) / channels
@@ -593,7 +614,10 @@
     token_rows = jnp.stack([tok_mean, inv_std, mean_gained, mean_both])
     token_rows = jnp.pad(token_rows, ((0, 4), (0, 0)))
     branch_seen = jnp.pad(branch_seen, ((0, 0), (0, width - classes)))
-    landed = scatter(n, conv_all, weights, pre_grad, token_rows, branch_seen)
+    landed, d_w_in, d_w_out = scatter(
+        n, conv_all, weights, pre_grad, token_rows, branch_seen,
+        norm_out, seen_narrow, scaled_head.astype(jnp.bfloat16),
+    )
     conv_grad = landed[:, :tok_count]
     my_seen = landed[:, tok_count : tok_count + class_count]
     d_head = dot(inputs_wide, logit_grad, (1, 1), fine)[:, :class_count] + my_scale[:, None] * my_seen

time: 174 us -> 175 us (level)
  matrix products: 19.7 us -> 12.2 us
  local copies, waits for them, and re-layouts: 12.6 us -> 18.7 us
  other arithmetic: 12.4 us -> 14.6 us
    dot_general x9 -> x7, matrix products: 15.9 us -> 8.42 us  [dot(): lax.dot_general(lhs, rhs, ((over[:1], over[1:]), ((), ())), precision=pre...]
    unnamed x53 -> x41, local copies, waits for them, and re-layouts: 9.78 us -> 16.2 us
    pallas_call x1, Pallas kernels: 44 us -> 37.9 us  [gather(): pl.pallas_call(functools.partial(gather_kernel, n), out_shape=(jax.ShapeD...]
    pallas_call x1, Pallas kernels: 44.3 us -> 48.9 us  [scatter(): pl.pallas_call(functools.partial(scatter_kernel, n), out_shape=(jax.Shape...]
    convert_element_type x0 -> x2, other arithmetic: none -> 4.08 us  [the longest x1 2.78 us: per_device(): scaled_head.astype(jnp.bfloat16)]
    mul x1 -> x0, other arithmetic: 2.35 us -> none  [per_device(): scaled_head = layer_scale[:, None] * head_pad.astype(jnp.float32)]
    reduce_sum x1, other arithmetic: 0.68 us -> 3.04 us  [per_device(): tok_mean = jnp.mean(conv_wide, axis=0)]
where the time goes in v3:
time: 175 us
  Pallas kernels  126 us (72%)
  local copies, waits for them, and re-layouts  18.7 us (11%)
  other arithmetic  14.6 us (8%)
  matrix products  12.2 us (7%)
  between operations  2.66 us (2%)
    pallas_call x1, Pallas kernels, scatter(): pl.pallas_call(functools.partial(scatter_kernel, n), out_shape=(jax.Shape...  48.9 us
    pallas_call x1, Pallas kernels, gather(): pl.pallas_call(functools.partial(gather_kernel, n), out_shape=(jax.ShapeD...  37.9 us
    pallas_call x1, Pallas kernels, total(): pl.pallas_call(functools.partial(total_kernel, n), out_shape=jax.ShapeDty...  23.2 us
    pallas_call x1, Pallas kernels, conv_back(): pl.pallas_call(conv_back_kernel, out_shape=(jax.ShapeDtypeStruct(grad.sha...  16.5 us
    unnamed x41, local copies, waits for them, and re-layouts  16.2 us
    dot_general x7, matrix products, dot(): lax.dot_general(lhs, rhs, ((over[:1], over[1:]), ((), ())), precision=pre...  8.42 us
    dot_general x1, matrix products, per_device(): pre_act = jnp.dot(w_in, norm_out, preferred_element_type=jnp.float32)  3.77 us

profile of v3, /device:TPU:0, one launch (start us, length us, event | category | flops | bytes accessed | tf_op | source)
XLA Modules:
  0.0 174.6 jit_solution(2625512294477233639)
XLA Ops:
  0.6 1.4 copy.24
  2.1 2.8 %fusion.21 = (bf16[2048,160]{1,0:T(8,128)(2,1)}, f32[2048,160]{1,0:T(8,128)}) fusion(bf16[2048,150]{1,0:T(8,128)(2,1)S(1)} %copy.24, f32[2048]{0:T(1024)} %param.11), kind=kLoop, calls=%fused_computation.53 | loop fusion | flops 983040 | bytes 2588672 | tf_op jit(solution)/shard_map/convert_element_type | solution.py:619
  4.8 0.7 copy.25.taps_ref
  5.6 37.9 %shard_map.135 = (bf16[2048,1024]{1,0:T(8,128)(2,1)}, f32[512,160]{1,0:T(8,128)}) custom-call(bf16[128,1024]{1,0:T(8,128)(2,1)} %x_ref.1, f32[128,49]{1,0:T(8,128)} %copy.25.taps_ref, bf16[512,2048]{1,0:T(8,128)(2,1)} %w_ref.1, f32[2048,160]{1,0:T(8,128)} %get-tuple-element.43.head_ref), custom_call_target="tpu_custom_call" | custom-call | tf_op jit(solution)/shard_map/pallas_call | solution.py:248
  43.5 3.0 %convert_reduce_fusion = f32[1024]{0:T(1024)S(1)} fusion(bf16[2048,1024]{1,0:T(8,128)(2,1)} %get-tuple-element.14.conv_ref), kind=kLoop, calls=%fused_computation.1 | loop fusion | flops 4193280 | bytes 4198400 | tf_op jit(solution)/shard_map/reduce_sum | solution.py:575
  46.9 1.1 fusion.2
  48.1 1.3 fusion.4.norm_ref
  49.7 3.8 %fusion.16 = (bf16[512,1024]{1,0:T(8,128)(2,1)S(1)}, f32[1024,512]{0,1:T(8,128)}) fusion(bf16[512,2048]{1,0:T(8,128)(2,1)S(1)} %copy-done.8, bf16[2048,1024]{1,0:T(8,128)(2,1)S(1)} %fusion.4.norm_ref), kind=kOutput, calls=%fused_computation.24 | convolution fusion | flops 2150105088 | bytes 9437184 | tf_op jit(solution)/shard_map/dot_general | solution.py:580
  53.4 0.6 fusion.22
  54.4 1.1 convolution_add_fusion.x_ref
  55.5 23.2 %shard_map.136 = f32[160,1024]{1,0:T(8,128)} custom-call(f32[160,1024]{1,0:T(8,128)} %convolution_add_fusion.x_ref), custom_call_target="tpu_custom_call" | custom-call | tf_op jit(solution)/shard_map/pallas_call | solution.py:359
  78.7 1.2 select_reduce_fusion.1
  79.9 1.4 select_reduce_fusion
  81.3 0.6 subtract_reduce_fusion
  82.5 1.9 %convolution_convert_fusion.1.unit_ref = bf16[512,160]{1,0:T(8,128)(2,1)S(1)} fusion(bf16[512,1024]{1,0:T(8,128)(2,1)S(1)} %get-tuple-element.46, f32[160,1024]{1,0:T(8,128)} %shard_map.136, s32[1024]{0:T(1024)S(1)} %copy-done.15, f32[1024]{0:T(1024)S(1)} %get-tuple-element.38, f32[1024]{0:T(1024)S(1)} %select_reduce_fusion.1, ...), kind=kOutput, calls=%fused_computation.29 | convolution fusion | flops 169000960 | bytes 1880224 | tf_op jit(solution)/shard_map/dot_general | solution.py:558
  84.4 0.7 copy-done.9
  86.2 1.1 pad.14.seen_ref
  87.3 3.0 %copy.26 = bf16[512,2048]{0,1:T(8,128)(2,1)S(1)} copy(bf16[512,2048]{1,0:T(8,128)(2,1)} %param.12) | data formatting | bytes 4194304 | tf_op args[4]
  90.4 1.9 %fusion.5 = (f32[512]{0:T(512)S(1)}, bf16[2048,512]{1,0:T(8,128)(2,1)}) fusion(bf16[512,2048]{0,1:T(8,128)(2,1)S(1)} %copy.26, f32[2048]{0:T(1024)S(1)} %copy-done.13), kind=kLoop, calls=%fused_computation.8 | loop fusion | flops 4193792 | bytes 4204544 | tf_op jit(solution)/shard_map/reduce_sum | solution.py:609
  92.3 0.8 copy-done.16
  93.1 3.2 %multiply_reduce_fusion = (f32[1024]{0:T(1024)S(1)}, f32[1024]{0:T(1024)S(1)}, bf16[512,1024]{1,0:T(8,128)(2,1)}) fusion(f32[512]{0:T(512)S(1)} %get-tuple-element.39, f32[1024,512]{0,1:T(8,128)S(1)} %copy-done.16, f32[512,160]{1,0:T(8,128)S(1)} %copy-done.12, f32[160,1024]{1,0:T(8,128)S(1)} %copy-done.4, s32[1024]{0:T(1024)S(1)} %copy-done.15, ...), kind=kOutput, calls=%fused_computation.26 | convolution fusion | flops 511637504 | bytes 4151456 | tf_op jit(solution)/shard_map/dot_general | solution.py:558
  96.3 0.6 select_maximum_fusion.rows_ref
  97.0 48.9 %shard_map.137 = (f32[128,1280]{1,0:T(8,128)}, f32[512,2048]{1,0:T(8,128)}, f32[512,2048]{1,0:T(8,128)}) custom-call(bf16[2048,1024]{1,0:T(8,128)(2,1)} %get-tuple-element.14.conv_ref, bf16[2048,512]{1,0:T(8,128)(2,1)} %get-tuple-element.40.w_ref, bf16[512,1024]{1,0:T(8,128)(2,1)} %get-tuple-element.41.p_ref, f32[8,1024]{1,0:T(8,128)} %select_maximum_fusion.rows_ref, ...), custom_call_target="tpu_custom_call" | custom-call | tf_op jit(solution)/shard_map/pallas_call | solution.py:528
  145.9 0.5 convolution_bitcast_fusion
  146.4 0.8 dynamic_slice.7
  147.2 0.6 slice_add_fusion
  147.8 0.7 copy.32
  148.6 0.6 fusion.20.add_ref
  149.4 16.5 %shard_map.138 = (f32[128,1024]{1,0:T(8,128)}, f32[128,49]{1,0:T(8,128)S(1)}) custom-call(f32[128,1024]{1,0:T(8,128)S(1)} %slice.15.grad_ref, f32[128,1024]{1,0:T(8,128)S(1)} %convert_element_type.64.x_ref, f32[128,49]{1,0:T(8,128)S(1)} %copy-done, f32[128,1024]{1,0:T(8,128)S(1)} %fusion.20.add_ref), custom_call_target="tpu_custom_call" | custom-call | tf_op jit(solution)/shard_map/pallas_call | solution.py:63
  165.9 0.7 copy.31
  166.6 4.8 %copy.37 = f32[512,2048]{1,0:T(8,128)} copy(f32[512,2048]{1,0:T(8,128)} %get-tuple-element.61) | data formatting | bytes 8388608
  171.5 2.0 %copy.38 = f32[512,2048]{1,0:T(8,128)} copy(f32[512,2048]{1,0:T(8,128)S(1)} %copy-done.6) | data formatting | bytes 8388608
  (40 shorter events, 2.4 us)
Async XLA Ops:
  2.0 2.8 %copy-start.14 = (f32[128,49]{0,1:T(8,128)S(1)}, f32[128,49]{0,1:T(8,128)}, u32[]{:S(2)}) copy-start(f32[128,49]{0,1:T(8,128)} %param.9) | copy-start | bytes 75268
  43.4 3.5 %copy-start.1 = (bf16[2048,1024]{1,0:T(8,128)(2,1)S(1)}, bf16[2048,1024]{1,0:T(8,128)(2,1)}, u32[]{:S(2)}) copy-start(bf16[2048,1024]{1,0:T(8,128)(2,1)} %get-tuple-element.14.conv_ref) | copy-start | bytes 12582916
  46.9 1.2 copy-start.13
  48.1 1.6 copy-start.8
  49.7 3.8 %copy-start.2 = (bf16[2048,1024]{1,0:T(8,128)(2,1)}, bf16[2048,1024]{1,0:T(8,128)(2,1)S(1)}, u32[]{:S(2)}) copy-start(bf16[2048,1024]{1,0:T(8,128)(2,1)S(1)} %fusion.4.norm_ref) | copy-start | bytes 12582916
  49.7 3.8 %copy-start.11 = (f32[512,160]{1,0:T(8,128)S(1)}, f32[512,160]{1,0:T(8,128)}, u32[]{:S(2)}) copy-start(f32[512,160]{1,0:T(8,128)} %get-tuple-element.15) | copy-start | bytes 983044
  53.4 1.0 copy-start.7
  54.4 25.5 %copy-start.15 = (s32[1024]{0:T(1024)S(1)}, s32[1024]{0:T(1024)}, u32[]{:S(2)}) copy-start(s32[1024]{0:T(1024)} %param.15) | copy-start | bytes 12292
  82.5 2.6 %copy-start.3 = (bf16[512,2048]{1,0:T(8,128)(2,1)S(1)}, bf16[512,2048]{1,0:T(8,128)(2,1)}, u32[]{:S(2)}) copy-start(bf16[512,2048]{1,0:T(8,128)(2,1)} %w_ref.1) | copy-start | bytes 6291460
  84.4 0.7 copy-start.9
  90.4 1.9 %copy-start.4 = (f32[160,1024]{1,0:T(8,128)S(1)}, f32[160,1024]{1,0:T(8,128)}, u32[]{:S(2)}) copy-start(f32[160,1024]{1,0:T(8,128)} %shard_map.136) | copy-start | bytes 1966084
  90.4 1.9 %copy-start.12 = (f32[512,160]{1,0:T(8,128)S(1)}, f32[512,160]{1,0:T(8,128)}, u32[]{:S(2)}) copy-start(f32[512,160]{1,0:T(8,128)} %get-tuple-element.15) | copy-start | bytes 983044
  90.4 2.7 %copy-start.16 = (f32[1024,512]{0,1:T(8,128)S(1)}, f32[1024,512]{0,1:T(8,128)}, u32[]{:S(2)}) copy-start(f32[1024,512]{0,1:T(8,128)} %get-tuple-element.47) | copy-start | bytes 6291460
  145.9 1.3 copy-start.10
  145.9 2.7 %copy-start.5 = (f32[160,1024]{1,0:T(8,128)S(1)}, f32[160,1024]{1,0:T(8,128)}, u32[]{:S(2)}) copy-start(f32[160,1024]{1,0:T(8,128)} %shard_map.136) | copy-start | bytes 1966084
  148.6 0.8 copy-start
  166.6 4.9 %copy-start.6 = (f32[512,2048]{1,0:T(8,128)S(1)}, f32[512,2048]{1,0:T(8,128)}, u32[]{:S(2)}) copy-start(f32[512,2048]{1,0:T(8,128)} %get-tuple-element.62) | copy-start | bytes 12582916

commit v4 on v3

--- a/solution.py
+++ b/solution.py
@@ -379,8 +379,7 @@
 
 
 def scatter_kernel(
-    n, conv_ref, w_ref, p_ref, rows_ref, seen_ref, norm_ref, unit_ref, head_ref,
-    out_ref, d_in_ref, d_out_ref,
+    n, conv_ref, w_ref, p_ref, rows_ref, seen_ref, out_ref,
     g_ref, t_in, y_in, u_in, d_in, y_out, z_out, t_sem, y_sem, u_sem, d_sem, zs_sem
 ):
     a = n // 4
@@ -428,8 +427,6 @@
         )
 
     tokens = conv_ref.shape[1]
-    slabs = min(a, 4)
-    deep = p_ref.shape[0] // slabs
     tok_mean, inv_std = rows_ref[0:1, :], rows_ref[1:2, :]
     mean_gained, mean_both = rows_ref[2:3, :], rows_ref[3:4, :]
 
@@ -466,10 +463,6 @@
             fill(order(k + 1), y, 1 - c)
             to_twin(order(k + 1), y, 1 - c).start()
             fill(order(k + 1), y, c)
-        if k < slabs:
-            slab = pl.ds(k * deep, deep)
-            d_in_ref[slab, :] = dot(p_ref[slab, :], norm_ref[...], (1, 1))
-            d_out_ref[slab, :] = dot(unit_ref[slab, :], head_ref[...], (1, 1))
         to_twin(zz, y, c).wait_recv()
         to_across(k, zz).wait_recv()
         term = (
@@ -522,18 +515,14 @@
             along(k, zz, u_in, u_sem, me).wait_send()
 
 
-def scatter(n, conv_all, weights, pre_grad, token_rows, seen, norm_out, units, head):
+def scatter(n, conv_all, weights, pre_grad, token_rows, seen):
     rows, cols = conv_all.shape[0] // n, conv_all.shape[1] + seen.shape[1]
     a = n // 4
     return pl.pallas_call(
         functools.partial(scatter_kernel, n),
-        out_shape=(
-            jax.ShapeDtypeStruct((rows, cols), jnp.float32),
-            jax.ShapeDtypeStruct((pre_grad.shape[0], norm_out.shape[0]), jnp.float32),
-            jax.ShapeDtypeStruct((units.shape[0], head.shape[0]), jnp.float32),
-        ),
-        in_specs=[pl.BlockSpec(memory_space=pltpu.VMEM)] * 8,
-        out_specs=(pl.BlockSpec(memory_space=pltpu.VMEM),) * 3,
+        out_shape=jax.ShapeDtypeStruct((rows, cols), jnp.float32),
+        in_specs=[pl.BlockSpec(memory_space=pltpu.VMEM)] * 5,
+        out_specs=pl.BlockSpec(memory_space=pltpu.VMEM),
         scratch_shapes=[
             pltpu.VMEM((n * rows, cols), jnp.bfloat16),
             pltpu.VMEM((n // 2, rows, cols), jnp.bfloat16),
@@ -551,7 +540,7 @@
         compiler_params=pltpu.CompilerParams(
             collective_id=2, has_side_effects=True, vmem_limit_bytes=VMEM_LIMIT
         ),
-    )(conv_all, weights, pre_grad, token_rows, seen, norm_out, units, head)
+    )(conv_all, weights, pre_grad, token_rows, seen)
 
 
 def dot(lhs, rhs, over, precision=None):
@@ -603,9 +592,11 @@
     seen = dot(hidden, grad_narrow, (1, 1))
     hidden_grad = dot(mixed, logit_grad, (1, 0), fine)
     seen_narrow = seen.astype(jnp.bfloat16)
+    d_w_out = dot(seen_narrow, scaled_head.astype(jnp.bfloat16), (1, 1))
     branch_seen = dot(w_out, seen_narrow, (0, 0)).astype(jnp.bfloat16)
     pre_grad_wide = hidden_grad * gelu_slope
     pre_grad = pre_grad_wide.astype(jnp.bfloat16)
+    d_w_in = dot(pre_grad, norm_out, (1, 1))
     gain_rows = jnp.sum(w_in.astype(jnp.float32) * norm_gain[None, :], axis=1)
     mean_gained = jnp.sum(gain_rows[:, None] * pre_grad_wide, axis=0) / channels
     mean_both = jnp.sum(pre_act * pre_grad_wide, axis=0) / channels
@@ -614,10 +605,7 @@
     token_rows = jnp.stack([tok_mean, inv_std, mean_gained, mean_both])
     token_rows = jnp.pad(token_rows, ((0, 4), (0, 0)))
     branch_seen = jnp.pad(branch_seen, ((0, 0), (0, width - classes)))
-    landed, d_w_in, d_w_out = scatter(
-        n, conv_all, weights, pre_grad, token_rows, branch_seen,
-        norm_out, seen_narrow, scaled_head.astype(jnp.bfloat16),
-    )
+    landed = scatter(n, conv_all, weights, pre_grad, token_rows, branch_seen)
     conv_grad = landed[:, :tok_count]
     my_seen = landed[:, tok_count : tok_count + class_count]
     d_head = dot(inputs_wide, logit_grad, (1, 1), fine)[:, :class_count] + my_scale[:, None] * my_seen

time: 175 us -> 170 us (0.971)
  matrix products: 12.2 us -> 19.7 us
  local copies, waits for them, and re-layouts: 18.7 us -> 12.8 us
  Pallas kernels: 126 us -> 122 us
  other arithmetic: 14.6 us -> 12.4 us
    dot_general x7 -> x9, matrix products: 8.42 us -> 15.9 us  [dot(): lax.dot_general(lhs, rhs, ((over[:1], over[1:]), ((), ())), precision=pre...]
    unnamed x41 -> x53, local copies, waits for them, and re-layouts: 16.2 us -> 9.78 us
    pallas_call x1, Pallas kernels: 48.9 us -> 44.1 us  [scatter(): pl.pallas_call(functools.partial(scatter_kernel, n), out_shape=jax.ShapeD...]
    convert_element_type x2 -> x0, other arithmetic: 4.08 us -> none  [the longest x1 2.78 us: per_device(): scaled_head.astype(jnp.bfloat16)]
    mul x0 -> x1, other arithmetic: none -> 2.35 us  [per_device(): scaled_head = layer_scale[:, None] * head_pad.astype(jnp.float32)]
    reduce_sum x1, other arithmetic: 3.04 us -> 0.68 us  [per_device(): tok_mean = jnp.mean(conv_wide, axis=0)]
where the time goes in v4:
time: 170 us; the launch traced here: 169 us
  Pallas kernels  122 us (72%)
  matrix products  19.7 us (12%)
  local copies, waits for them, and re-layouts  12.8 us (8%)
  other arithmetic  12.4 us (7%)
  between operations  2.7 us (2%)
    pallas_call x1, Pallas kernels, scatter(): pl.pallas_call(functools.partial(scatter_kernel, n), out_shape=jax.ShapeD...  44.1 us
    pallas_call x1, Pallas kernels, gather(): pl.pallas_call(functools.partial(gather_kernel, n), out_shape=(jax.ShapeD...  37.9 us
    pallas_call x1, Pallas kernels, total(): pl.pallas_call(functools.partial(total_kernel, n), out_shape=jax.ShapeDty...  23.2 us
    pallas_call x1, Pallas kernels, conv_back(): pl.pallas_call(conv_back_kernel, out_shape=(jax.ShapeDtypeStruct(grad.sha...  16.5 us
    dot_general x9, matrix products, dot(): lax.dot_general(lhs, rhs, ((over[:1], over[1:]), ((), ())), precision=pre...  15.9 us
    unnamed x53, local copies, waits for them, and re-layouts  9.78 us
    dot_general x1, matrix products, per_device(): pre_act = jnp.dot(w_in, norm_out, preferred_element_type=jnp.float32)  3.81 us

profile of v4, /device:TPU:0, one launch (start us, length us, event | category | flops | bytes accessed | tf_op | source)
XLA Modules:
  0.0 169.2 jit_solution(17507642800510824985)
XLA Ops:
  0.6 1.5 copy.24.taps_ref
  2.1 1.4 copy.23
  3.5 2.4 %convert_multiply_fusion.1.head_ref = f32[2048,160]{1,0:T(8,128)} fusion(f32[2048]{0:T(1024)} %param.11, bf16[2048,150]{1,0:T(8,128)(2,1)S(1)} %copy.23), kind=kLoop, calls=%fused_computation.27 | loop fusion | flops 655360 | bytes 1933312 | tf_op jit(solution)/shard_map/mul | solution.py:561
  5.9 37.9 %shard_map.135 = (bf16[2048,1024]{1,0:T(8,128)(2,1)}, f32[512,160]{1,0:T(8,128)}) custom-call(bf16[128,1024]{1,0:T(8,128)(2,1)} %x_ref.1, f32[128,49]{1,0:T(8,128)} %copy.24.taps_ref, bf16[512,2048]{1,0:T(8,128)(2,1)} %w_ref.1, f32[2048,160]{1,0:T(8,128)} %convert_multiply_fusion.1.head_ref), custom_call_target="tpu_custom_call" | custom-call | tf_op jit(solution)/shard_map/pallas_call | solution.py:248
  43.8 2.9 %copy.25 = bf16[512,2048]{0,1:T(8,128)(2,1)S(1)} copy(bf16[512,2048]{1,0:T(8,128)(2,1)} %param.12) | data formatting | bytes 4194304 | tf_op args[4]
  46.6 2.4 %fusion.5 = (f32[512]{0:T(512)}, bf16[2048,512]{1,0:T(8,128)(2,1)}) fusion(bf16[512,2048]{0,1:T(8,128)(2,1)S(1)} %copy.25, f32[2048]{0:T(1024)S(1)} %copy-done.16), kind=kLoop, calls=%fused_computation.8 | loop fusion | flops 4193792 | bytes 4204544 | tf_op jit(solution)/shard_map/reduce_sum | solution.py:600
  49.6 0.7 convert_reduce_fusion
  50.3 1.2 fusion.2
  51.9 3.8 %fusion.16 = (bf16[512,1024]{1,0:T(8,128)(2,1)S(1)}, f32[1024,512]{0,1:T(8,128)}) fusion(bf16[512,2048]{1,0:T(8,128)(2,1)S(1)} %copy-done.7, bf16[2048,1024]{1,0:T(8,128)(2,1)S(1)} %copy-done.1, f32[1024]{0:T(1024)S(1)} %add_rsqrt_fusion, f32[1024]{0:T(1024)S(1)} %broadcast_multiply_fusion.2, f32[2048]{0:T(1024)S(1)} %copy-done.16), kind=kOutput, calls=%fused_computation.24 | convolution fusion | flops 2160590848 | bytes 9453568 | tf_op jit(solution)/shard_map/dot_general | solution.py:569
  55.7 0.6 fusion.27
  56.6 1.1 convolution_add_fusion.x_ref
  57.8 23.2 %shard_map.136 = f32[160,1024]{1,0:T(8,128)} custom-call(f32[160,1024]{1,0:T(8,128)} %convolution_add_fusion.x_ref), custom_call_target="tpu_custom_call" | custom-call | tf_op jit(solution)/shard_map/pallas_call | solution.py:359
  81.0 1.2 select_reduce_fusion.1
  82.2 1.3 select_reduce_fusion
  83.6 4.4 %multiply_reduce_fusion = (f32[1024]{0:T(1024)S(1)}, f32[1024]{0:T(1024)S(1)}, bf16[512,1024]{1,0:T(8,128)(2,1)}) fusion(f32[512]{0:T(512)S(1)} %copy-done.20, f32[1024,512]{0,1:T(8,128)S(1)} %copy-done.23, f32[512,160]{1,0:T(8,128)S(1)} %copy-done.11, f32[160,1024]{1,0:T(8,128)} %shard_map.136, s32[1024]{0:T(1024)S(1)} %copy-done.18, ...), kind=kOutput, calls=%fused_computation.26 | convolution fusion | flops 511637504 | bytes 4151456 | tf_op jit(solution)/shard_map/dot_general | solution.py:547
  88.0 0.6 select_maximum_fusion.rows_ref
  88.6 0.6 convolution_convert_fusion.1
  89.2 0.7 copy-done.9
  90.3 0.5 convolution_convert_fusion
  90.8 0.7 copy.26
  91.5 1.2 pad.14.seen_ref
  92.7 44.1 %shard_map.137 = f32[128,1280]{1,0:T(8,128)} custom-call(bf16[2048,1024]{1,0:T(8,128)(2,1)} %get-tuple-element.11.conv_ref, bf16[2048,512]{1,0:T(8,128)(2,1)} %get-tuple-element.34.w_ref, bf16[512,1024]{1,0:T(8,128)(2,1)} %get-tuple-element.35.p_ref, f32[8,1024]{1,0:T(8,128)} %select_maximum_fusion.rows_ref, bf16[2048,256]{1,0:T(8,128)(2,1)} %pad.14.seen_ref), custom_call_target="tpu_custom_call" | custom-call | tf_op jit(solution)/shard_map/pallas_call | solution.py:521
  136.7 1.1 slice.15.grad_ref
  137.9 0.6 fusion.26.add_ref
  138.7 16.5 %shard_map.138 = (f32[128,1024]{1,0:T(8,128)}, f32[128,49]{1,0:T(8,128)S(1)}) custom-call(f32[128,1024]{1,0:T(8,128)S(1)} %slice.15.grad_ref, f32[128,1024]{1,0:T(8,128)S(1)} %convert_element_type.63.x_ref, f32[128,49]{1,0:T(8,128)S(1)} %copy-done, f32[128,1024]{1,0:T(8,128)S(1)} %fusion.26.add_ref), custom_call_target="tpu_custom_call" | custom-call | tf_op jit(solution)/shard_map/pallas_call | solution.py:63
  155.2 0.7 copy.29
  155.9 0.5 convolution_bitcast_fusion
  156.5 1.8 %slice_add_fusion = (f32[128,150]{1,0:T(8,128)S(1)}, f32[128]{0:T(128)}) fusion(f32[128,160]{1,0:T(8,128)S(1)} %convolution_bitcast_fusion, f32[128,1280]{1,0:T(8,128)} %shard_map.137, f32[128]{0:T(128)S(1)} %dynamic_slice.7, s32[]{:T(128)S(6)} %select_n.11, bf16[2048,150]{1,0:T(8,128)(2,1)S(1)} %copy.23), kind=kLoop, calls=%fused_computation.44 | loop fusion | flops 95872 | bytes 845828 | tf_op jit(solution)/shard_map/add | solution.py:611
  158.4 4.6 %fusion.20 = f32[512,2048]{1,0:T(8,128)} fusion(bf16[512,1024]{1,0:T(8,128)(2,1)S(1)} %copy-done.8, bf16[2048,1024]{1,0:T(8,128)(2,1)S(1)} %copy-done.2, f32[1024]{0:T(1024)S(1)} %copy-done.15, f32[1024]{0:T(1024)S(1)} %broadcast_multiply_fusion.2, f32[2048]{0:T(1024)S(1)} %copy-done.17), kind=kOutput, calls=%fused_computation.35 | convolution fusion | flops 2157969408 | bytes 9453568 | tf_op jit(solution)/shard_map/dot_general | solution.py:547
  163.0 3.1 %fusion.18 = f32[512,2048]{1,0:T(8,128)} fusion(bf16[512,160]{0,1:T(8,128)(2,1)S(1)} %copy-done.10, f32[2048]{0:T(1024)S(1)} %copy-done.12, bf16[2048,150]{1,0:T(8,128)(2,1)S(1)} %copy.23), kind=kOutput, calls=%fused_computation.31 | convolution fusion | flops 336527360 | bytes 4980736 | tf_op jit(solution)/shard_map/dot_general | solution.py:547
  166.1 0.7 copy.30
  166.8 0.6 subtract_reduce_fusion
  (53 shorter events, 2.1 us)
Async XLA Ops:
  43.7 2.9 %copy-start.16 = (f32[2048]{0:T(1024)S(1)}, f32[2048]{0:T(1024)}, u32[]{:S(2)}) copy-start(f32[2048]{0:T(1024)} %param.10) | copy-start | bytes 24580
  46.6 2.9 %copy-start.1 = (bf16[2048,1024]{1,0:T(8,128)(2,1)S(1)}, bf16[2048,1024]{1,0:T(8,128)(2,1)}, u32[]{:S(2)}) copy-start(bf16[2048,1024]{1,0:T(8,128)(2,1)} %get-tuple-element.11.conv_ref) | copy-start | bytes 12582916
  50.3 1.6 copy-start.7
  51.9 3.8 %copy-start.13 = (f32[1024]{0:T(1024)}, f32[1024]{0:T(1024)S(1)}, u32[]{:S(2)}) copy-start(f32[1024]{0:T(1024)S(1)} %add_rsqrt_fusion) | copy-start | bytes 12292
  51.9 3.8 %copy-start.11 = (f32[512,160]{1,0:T(8,128)S(1)}, f32[512,160]{1,0:T(8,128)}, u32[]{:S(2)}) copy-start(f32[512,160]{1,0:T(8,128)} %get-tuple-element.12) | copy-start | bytes 983044
  55.7 1.0 copy-start.5
  56.6 25.6 %copy-start.18 = (s32[1024]{0:T(1024)S(1)}, s32[1024]{0:T(1024)}, u32[]{:S(2)}) copy-start(s32[1024]{0:T(1024)} %param.15) | copy-start | bytes 12292
  56.6 26.9 %copy-start.20 = (f32[512]{0:T(512)S(1)}, f32[512]{0:T(512)}, u32[]{:S(2)}) copy-start(f32[512]{0:T(512)} %get-tuple-element.33) | copy-start | bytes 6148
  56.6 26.9 %copy-start.23 = (f32[1024,512]{0,1:T(8,128)S(1)}, f32[1024,512]{0,1:T(8,128)}, u32[]{:S(2)}) copy-start(f32[1024,512]{0,1:T(8,128)} %get-tuple-element.39) | copy-start | bytes 6291460
  81.0 7.7 %copy-start.21 = (pred[160]{0:T(512)(128)(4,1)}, pred[160]{0:T(512)(128)(4,1)S(1)}, u32[]{:S(2)}) copy-start(pred[160]{0:T(512)(128)(4,1)S(1)} %iota_compare_fusion.2) | copy-start | bytes 484
  83.6 4.4 %copy-start.14 = (f32[1024]{0:T(1024)S(1)}, f32[1024]{0:T(1024)}, u32[]{:S(2)}) copy-start(f32[1024]{0:T(1024)} %copy-done.13) | copy-start | bytes 12292
  83.6 5.0 %copy-start.4 = (f32[160,1024]{1,0:T(8,128)S(1)}, f32[160,1024]{1,0:T(8,128)}, u32[]{:S(2)}) copy-start(f32[160,1024]{1,0:T(8,128)} %shard_map.136) | copy-start | bytes 1966084
  88.6 1.7 copy-start.3
  89.2 0.7 copy-start.9
  92.7 45.2 %copy-start.6 = (bf16[128,1024]{1,0:T(8,128)(2,1)S(1)}, bf16[128,1024]{1,0:T(8,128)(2,1)}, u32[]{:S(2)}) copy-start(bf16[128,1024]{1,0:T(8,128)(2,1)} %x_ref.1) | copy-start | bytes 786436
  92.7 45.3 %copy-start.19 = (s32[1024]{0:T(1024)S(1)}, s32[1024]{0:T(1024)}, u32[]{:S(2)}) copy-start(s32[1024]{0:T(1024)} %param.15) | copy-start | bytes 12292
  92.7 45.3 %copy-start.22 = (pred[160]{0:T(512)(128)(4,1)S(1)}, pred[160]{0:T(512)(128)(4,1)}, u32[]{:S(2)}) copy-start(pred[160]{0:T(512)(128)(4,1)} %copy-done.21) | copy-start | bytes 484
  137.8 0.8 copy-start
  138.7 19.7 %copy-start.8 = (bf16[512,1024]{1,0:T(8,128)(2,1)S(1)}, bf16[512,1024]{1,0:T(8,128)(2,1)}, u32[]{:S(2)}) copy-start(bf16[512,1024]{1,0:T(8,128)(2,1)} %get-tuple-element.35.p_ref) | copy-start | bytes 3145732
  155.2 1.2 copy-start.12
  155.9 2.5 %copy-start.2 = (bf16[2048,1024]{1,0:T(8,128)(2,1)S(1)}, bf16[2048,1024]{1,0:T(8,128)(2,1)}, u32[]{:S(2)}) copy-start(bf16[2048,1024]{1,0:T(8,128)(2,1)} %get-tuple-element.11.conv_ref) | copy-start | bytes 12582916
  155.9 2.5 %copy-start.15 = (f32[1024]{0:T(1024)S(1)}, f32[1024]{0:T(1024)}, u32[]{:S(2)}) copy-start(f32[1024]{0:T(1024)} %copy-done.13) | copy-start | bytes 12292
  155.9 2.5 %copy-start.17 = (f32[2048]{0:T(1024)S(1)}, f32[2048]{0:T(1024)}, u32[]{:S(2)}) copy-start(f32[2048]{0:T(1024)} %param.10) | copy-start | bytes 24580
  158.4 4.6 %copy-start.10 = (bf16[512,160]{0,1:T(8,128)(2,1)S(1)}, bf16[512,160]{0,1:T(8,128)(2,1)}, u32[]{:S(2)}) copy-start(bf16[512,160]{0,1:T(8,128)(2,1)} %copy-done.9) | copy-start | bytes 491524
